TPU v7x, 1024 devices: a whole 8x8x8 slice. The times are simulated.
1024 devices in a mesh: ctx: 128 (over x, y, z_hi), head: 8 (over z_lo, core).
Axes of the slice: x: 8, y: 8, z: 8 (z_hi: 2, z_lo: 4; z = z_hi * 4 + z_lo), core: 2. Of those that a mesh axis runs over, the one named last changes fastest.
Arguments:
- query_nope: bfloat16 [16384, 8192], P('ctx', 'head'), may hold values from -6 to 6
- query_rope: bfloat16 [16384, 4096], P('ctx', 'head'), may hold values from -450 to 450
- grad_out: bfloat16 [16384, 8192], P('ctx', 'head'), may hold values from -24 to 24
- latent: bfloat16 [16384, 576], P(('ctx', 'head')), may hold values from -8 to 8
- key_up: bfloat16 [512, 8192], P(None, 'head'), may hold values from -0.25 to 0.25
- value_up: bfloat16 [512, 8192], P(None, 'head'), may hold values from -0.25 to 0.25
- block_keep: int32 [128, 3], P('ctx'), may hold values 0 or 1
Outputs:
- d_query_nope: float32 [16384, 8192], P('ctx', 'head')
- d_query_rope: float32 [16384, 4096], P('ctx', 'head')
- d_latent: float32 [16384, 576], P(('ctx', 'head'))
All inputs are finite; a program needn't handle non-finite values. No bound on the sum of `block_keep` on one device may be relied on, other than what follows from the above.
Results may differ from a plain program's by a relative error of at most 0.015.
Values may be sent and summed in bfloat16 or wider, within the bound.
No kernel may reach another device: no remote copies, remote signals or barrier semaphores. Data moves between devices by JAX's collectives and lax.ppermute only.
A program may use at most 32 MiB of HBM per device.

v0:
```python
import math

import jax
import jax.numpy as jnp
from jax import lax
from jax.sharding import PartitionSpec as P

NOPE = 128
ROPE = 64
VDIM = 128
RANK = 512


def laid_out(blocks, dim):
    lengths = list(blocks.shape[1:])
    lengths[dim] *= blocks.shape[0]
    return jnp.moveaxis(blocks, 0, dim).reshape(lengths)


def from_everyone(array, axis):
    copies = jnp.broadcast_to(array, (lax.axis_size(axis), *array.shape))
    return lax.all_to_all(copies, axis, split_axis=0, concat_axis=0, tiled=True)


def gather_directly(array, axis, dim):
    return laid_out(from_everyone(array, axis), dim)


def shifted(block, axis, distance):
    devices = range(lax.axis_size(axis))
    route = [(i - distance, i) for i in devices if i - distance in devices]
    return lax.ppermute(block, axis, route)


def in_blocks(array, dim, length):
    lengths = array.shape
    blocks = array.reshape(*lengths[:dim], length, lengths[dim] // length, *lengths[dim + 1 :])
    return jnp.moveaxis(blocks, dim, 0)


def summed_on_arrival(array, axis, dim):
    length = lax.axis_size(axis)
    blocks = lax.all_to_all(in_blocks(array, dim, length), axis, 0, 0, tiled=True)
    return jnp.sum(blocks, axis=0)


def window_mask(group_len, cycle_steps, keep_row, position):
    grid_shape = (group_len, cycle_steps + 1, group_len)
    query_at = lax.broadcasted_iota(jnp.int32, grid_shape, 0)
    block_at = lax.broadcasted_iota(jnp.int32, grid_shape, 1)
    key_at = lax.broadcasted_iota(jnp.int32, grid_shape, 2)
    blocks_back = cycle_steps - block_at
    block_flags = jnp.concatenate([keep_row[::-1], jnp.ones((1,), jnp.int32)])
    kept_block = block_flags[None, :, None] == 1
    in_range = position - blocks_back >= 0
    causal = (blocks_back > 0) | (key_at <= query_at)
    return (kept_block & in_range & causal).reshape(group_len, (cycle_steps + 1) * group_len)


def block_grads(query_nope, query_rope, grad_out, window, key_up, value_up, allowed):
    group_len = query_nope.shape[0]
    window_len = window.shape[0]
    head_count = key_up.shape[1] // NOPE
    score_scale = 1.0 / math.sqrt(NOPE + ROPE)
    content = window[:, :RANK]
    rope_keys = window[:, RANK:]
    key_heads = (
        jnp.dot(content, key_up, preferred_element_type=jnp.float32)
        .astype(jnp.bfloat16)
        .reshape(window_len, head_count, NOPE)
    )
    value_heads = (
        jnp.dot(content, value_up, preferred_element_type=jnp.float32)
        .astype(jnp.bfloat16)
        .reshape(window_len, head_count, VDIM)
    )
    query_heads = query_nope.reshape(group_len, head_count, NOPE)
    rope_heads = query_rope.reshape(group_len, head_count, ROPE)
    out_heads = grad_out.reshape(group_len, head_count, VDIM)
    scores = (
        jnp.einsum("chd,khd->hck", query_heads, key_heads, preferred_element_type=jnp.float32)
        + jnp.einsum("chd,kd->hck", rope_heads, rope_keys, preferred_element_type=jnp.float32)
    ) * score_scale
    scores = jnp.where(allowed[None], scores, -jnp.inf)
    row_top = jnp.max(scores, axis=2, keepdims=True)
    exponent = jnp.exp(scores - row_top)
    probs = exponent / jnp.sum(exponent, axis=2, keepdims=True)
    weights = probs.astype(jnp.bfloat16)
    output = jnp.einsum("hck,khd->chd", weights, value_heads, preferred_element_type=jnp.float32)
    row_delta = jnp.sum(output * out_heads, axis=2)
    slopes = jnp.einsum("chd,khd->hck", out_heads, value_heads, preferred_element_type=jnp.float32)
    score_grad = (probs * (slopes - row_delta.T[:, :, None]) * score_scale).astype(jnp.bfloat16)
    query_grad_nope = jnp.einsum(
        "hck,khd->chd", score_grad, key_heads, preferred_element_type=jnp.float32
    ).reshape(group_len, head_count * NOPE)
    query_grad_rope = jnp.einsum(
        "hck,kd->chd", score_grad, rope_keys, preferred_element_type=jnp.float32
    ).reshape(group_len, head_count * ROPE)
    key_grad = (
        jnp.einsum("hck,chd->khd", score_grad, query_heads, preferred_element_type=jnp.float32)
        .astype(jnp.bfloat16)
        .reshape(window_len, head_count * NOPE)
    )
    rope_grad = jnp.einsum(
        "hck,chd->kd", score_grad, rope_heads, preferred_element_type=jnp.float32
    )
    value_grad = (
        jnp.einsum("hck,chd->khd", weights, out_heads, preferred_element_type=jnp.float32)
        .astype(jnp.bfloat16)
        .reshape(window_len, head_count * VDIM)
    )
    content_grad = jnp.dot(key_grad, key_up.T, preferred_element_type=jnp.float32) + jnp.dot(
        value_grad, value_up.T, preferred_element_type=jnp.float32
    )
    return (query_grad_nope, query_grad_rope, jnp.concatenate([content_grad, rope_grad], axis=1))


def on_device(query_nope, query_rope, grad_out, latent, key_up, value_up, block_keep):
    group_len = query_nope.shape[0]
    cycle_steps = block_keep.shape[1]
    width = latent.shape[1]
    position = lax.axis_index("ctx")
    gathered = gather_directly(latent, "head", 0)
    blocks = [gathered]
    for cycle_step in range(1, cycle_steps + 1):
        source = gathered
        blocks.append(shifted(source, "ctx", cycle_step))
    window = jnp.concatenate(blocks[::-1], axis=0)
    allowed = window_mask(group_len, cycle_steps, block_keep[0], position)
    grad_nope, grad_rope, partial_value = block_grads(
        query_nope, query_rope, grad_out, window, key_up, value_up, allowed
    )
    partial_value = partial_value.reshape(cycle_steps + 1, group_len, width)
    carried = partial_value[cycle_steps]
    for cycle_step in range(1, cycle_steps + 1):
        source = partial_value[cycle_steps - cycle_step]
        arrived = shifted(source, "ctx", -cycle_step)
        carried = arrived + carried
    d_latent = summed_on_arrival(carried, "head", 0)
    return (grad_nope, grad_rope, d_latent)


def solution(mesh):
    placed = (
        P("ctx", "head"),
        P("ctx", "head"),
        P("ctx", "head"),
        P(("ctx", "head"), None),
        P(None, "head"),
        P(None, "head"),
        P("ctx", None),
    )
    return jax.shard_map(
        on_device,
        mesh=mesh,
        in_specs=placed,
        out_specs=(P("ctx", "head"), P("ctx", "head"), P(("ctx", "head"), None)),
        check_vma=False,
    )
```

profile of v0, /device:TPU:40, one launch (start us, length us, event | category | flops | bytes accessed | tf_op | source)
XLA Modules:
  0.0 136.2 jit_solution(8079558490657050151)
XLA Ops:
  0.6 1.5 %broadcast_in_dim.19 = bf16[8,16,576]{2,1,0:T(8,128)(2,1)} broadcast(bf16[16,576]{1,0:T(8,128)(2,1)} %param.10), dimensions={1,2} | broadcast | bytes 165888 | tf_op jit(solution)/shard_map/broadcast_in_dim | solution.py:21
  2.1 10.0 %all-to-all-start = ((bf16[8,16,576]{2,1,0:T(8,128)(2,1)}), bf16[8,16,576]{2,1,0:T(8,128)(2,1)S(1)}, u32[]{:S(2)}, u32[]{:S(2)}) async-start(bf16[8,16,576]{2,1,0:T(8,128)(2,1)} %broadcast_in_dim.19), calls=%async_computation | async-start | bytes 327680 | tf_op jit(solution)/shard_map/all_to_all | solution.py:22
  15.1 1.8 %copy.36 = bf16[128,1024]{0,1:T(8,128)(2,1)} copy(bf16[128,1024]{1,0:T(8,128)(2,1)} %param.9) | data formatting | bytes 524288 | tf_op args[2]
  17.0 2.3 %all-to-all-done = bf16[8,16,576]{2,1,0:T(8,128)(2,1)S(1)} async-done(((bf16[8,16,576]{2,1,0:T(8,128)(2,1)}), bf16[8,16,576]{2,1,0:T(8,128)(2,1)S(1)}, u32[]{:S(2)}, u32[]{:S(2)}) %all-to-all-start) | async-done | bytes 147488 | tf_op jit(solution)/shard_map/all_to_all | solution.py:22
  19.5 11.9 %collective-permute-start.2 = (bf16[128,576]{0,1:T(8,128)(2,1)S(1)}, bf16[128,576]{0,1:T(8,128)(2,1)S(1)}, u32[]{:S(2)}, u32[]{:S(2)}) collective-permute-start(bf16[128,576]{0,1:T(8,128)(2,1)S(1)} %copy.29), channel_id=1, source_target_pairs={{0,8},{8,16},{16,24},{24,32},{32,40},{40,48},{48,56},{56,64},{64,7... | collective-permute-start | bytes 442376 | tf_op jit(solution)/shard_map/ppermute | solution.py:32
  31.4 3.6 %collective-permute-start.1 = (bf16[128,576]{0,1:T(8,128)(2,1)S(1)}, bf16[128,576]{0,1:T(8,128)(2,1)S(1)}, u32[]{:S(2)}, u32[]{:S(2)}) collective-permute-start(bf16[128,576]{0,1:T(8,128)(2,1)S(1)} %copy.29), channel_id=1, source_target_pairs={{0,16},{8,24},{16,32},{24,40},{32,48},{40,56},{48,64},{56,72},{64,... | collective-permute-start | bytes 442376 | tf_op jit(solution)/shard_map/ppermute | solution.py:32
  35.0 4.3 %collective-permute-start = (bf16[128,576]{0,1:T(8,128)(2,1)S(1)}, bf16[128,576]{0,1:T(8,128)(2,1)S(1)}, u32[]{:S(2)}, u32[]{:S(2)}) collective-permute-start(bf16[128,576]{0,1:T(8,128)(2,1)S(1)} %copy.29), channel_id=1, source_target_pairs={{0,24},{8,32},{16,40},{24,48},{32,56},{40,64},{48,72},{56,80},{64,... | collective-permute-start | bytes 442376 | tf_op jit(solution)/shard_map/ppermute | solution.py:32
  39.5 9.7 %collective-permute-done = bf16[128,576]{0,1:T(8,128)(2,1)S(1)} collective-permute-done((bf16[128,576]{0,1:T(8,128)(2,1)S(1)}, bf16[128,576]{0,1:T(8,128)(2,1)S(1)}, u32[]{:S(2)}, u32[]{:S(2)}) %collective-permute-start) | collective-permute-done | bytes 147488 | tf_op jit(solution)/shard_map/ppermute | solution.py:32
  50.2 1.9 %convolution_convert_fusion.2 = bf16[512,1024]{1,0:T(8,128)(2,1)S(1)} fusion(bf16[512,1024]{1,0:T(8,128)(2,1)} %param.12, bf16[512,576]{0,1:T(8,128)(2,1)S(1)} %pad_maximum_fusion), kind=kOutput, calls=%fused_computation.13 | convolution fusion | flops 537395200 | bytes 2621440 | tf_op jit(solution)/shard_map/dot_general | solution.py:73
  53.5 2.7 %convolution_convert_fusion.3 = bf16[512,1024]{1,0:T(8,128)(2,1)} fusion(bf16[512,1024]{1,0:T(8,128)(2,1)S(1)} %copy-done, bf16[512,576]{0,1:T(8,128)(2,1)} %copy-done.7), kind=kOutput, calls=%fused_computation.14 | convolution fusion | flops 537395200 | bytes 2621440 | tf_op jit(solution)/shard_map/dot_general | solution.py:68
  58.9 2.0 %fusion.21 = (f32[8,128]{1,0:T(8,128)S(1)}, f32[8,128,512]{1,2,0:T(8,128)}) fusion(f32[8,128,512]{1,2,0:T(8,128)S(1)} %fusion.4), kind=kOutput, calls=%fused_computation.45 | output fusion | flops 1049087 | bytes 4198400 | tf_op jit(solution)/shard_map/sub | solution.py:86
  60.8 4.1 %convolution_convert_fusion = bf16[8,512,128]{1,2,0:T(8,128)(2,1)} fusion(bf16[128,8,128]{0,2,1:T(8,128)(2,1)} %bitcast.90, f32[8,128]{1,0:T(8,128)S(1)} %get-tuple-element.12, f32[8,128,512]{1,2,0:T(8,128)} %copy-done.1), kind=kOutput, calls=%fused_computation.11 | convolution fusion | flops 136316416 | bytes 3411968 | tf_op jit(solution)/shard_map/hck,chd->khd/dot_general | solution.py:108
  65.0 3.1 %fusion.6 = f32[128,8]{0,1:T(8,128)S(1)} fusion(bf16[512,8,128]{0,2,1:T(8,128)(2,1)S(1)} %bitcast.85, bf16[128,8,128]{0,2,1:T(8,128)(2,1)} %bitcast.91, f32[8,128]{1,0:T(8,128)S(1)} %get-tuple-element.12, f32[8,128,512]{1,2,0:T(8,128)} %copy-done.1), kind=kOutput, calls=%fused_computation.18 | convolution fusion | flops 136184320 | bytes 3416064 | tf_op jit(solution)/shard_map/hck,khd->chd/dot_general | solution.py:89
  68.1 2.6 %fusion.2 = bf16[8,128,512]{1,2,0:T(8,128)(2,1)S(1)} fusion(bf16[512,8,128]{0,2,1:T(8,128)(2,1)} %bitcast.84, bf16[128,8,128]{0,2,1:T(8,128)(2,1)} %bitcast.92, f32[8,128]{1,0:T(8,128)S(1)} %bitcast.94, f32[8,128,512]{1,2,0:T(8,128)} %get-tuple-element.13, f32[8,128]{1,0:T(8,128)S(1)} %get-tuple-element.12), kind=kOutput, calls=%fused_computation.3 | convolution fusion | flops 136839168 | bytes 4464640 | tf_op jit(solution)/shard_map/chd,khd->hck/dot_general | solution.py:91
  73.9 2.6 %collective-permute-start.5 = (f32[128,576]{0,1:T(8,128)S(1)}, f32[128,576]{0,1:T(8,128)S(1)}, u32[]{:S(2)}, u32[]{:S(2)}) collective-permute-start(f32[128,576]{0,1:T(8,128)S(1)} %get-tuple-element.9), channel_id=1, source_target_pairs={{8,0},{16,8},{24,16},{32,24},{40,32},{48,40},{56,48},{64,56},{72,6... | collective-permute-start | bytes 884744 | tf_op jit(solution)/shard_map/ppermute | solution.py:32
  76.6 11.0 %collective-permute-start.3 = (f32[128,576]{0,1:T(8,128)S(1)}, f32[128,576]{0,1:T(8,128)S(1)}, u32[]{:S(2)}, u32[]{:S(2)}) collective-permute-start(f32[128,576]{0,1:T(8,128)S(1)} %get-tuple-element.10), channel_id=1, source_target_pairs={{24,0},{32,8},{40,16},{48,24},{56,32},{64,40},{72,48},{80,56},{88,... | collective-permute-start | bytes 884744 | tf_op jit(solution)/shard_map/ppermute | solution.py:32
  87.6 2.9 %collective-permute-start.4 = (f32[128,576]{0,1:T(8,128)S(1)}, f32[128,576]{0,1:T(8,128)S(1)}, u32[]{:S(2)}, u32[]{:S(2)}) collective-permute-start(f32[128,576]{0,1:T(8,128)S(1)} %get-tuple-element.11), channel_id=1, source_target_pairs={{16,0},{24,8},{32,16},{40,24},{48,32},{56,40},{64,48},{72,56},{80,... | collective-permute-start | bytes 884744 | tf_op jit(solution)/shard_map/ppermute | solution.py:32
  90.5 13.3 %collective-permute-done.5 = f32[128,576]{0,1:T(8,128)S(1)} collective-permute-done((f32[128,576]{0,1:T(8,128)S(1)}, f32[128,576]{0,1:T(8,128)S(1)}, u32[]{:S(2)}, u32[]{:S(2)}) %collective-permute-start.5) | collective-permute-done | bytes 294944 | tf_op jit(solution)/shard_map/ppermute | solution.py:32
  103.8 12.8 %collective-permute-done.4 = f32[128,576]{0,1:T(8,128)S(1)} collective-permute-done((f32[128,576]{0,1:T(8,128)S(1)}, f32[128,576]{0,1:T(8,128)S(1)}, u32[]{:S(2)}, u32[]{:S(2)}) %collective-permute-start.4) | collective-permute-done | bytes 294944 | tf_op jit(solution)/shard_map/ppermute | solution.py:32
  117.4 1.9 %copy.48 = f32[128,576]{1,0:T(8,128)} copy(f32[128,576]{0,1:T(8,128)} %fusion.15) | data formatting | bytes 589824 | tf_op jit(solution)/shard_map/add | solution.py:138
  119.3 4.2 %all-to-all-start.1 = ((f32[8,16,576]{2,1,0:T(8,128)}), f32[8,16,576]{2,1,0:T(8,128)}, u32[]{:S(2)}, u32[]{:S(2)}) async-start(f32[8,16,576]{2,1,0:T(8,128)} %bitcast.81), calls=%async_computation.1 | async-start | bytes 655360 | tf_op jit(solution)/shard_map/all_to_all | solution.py:43
  124.7 2.0 %copy.49 = f32[128,1024]{1,0:T(8,128)} copy(f32[128,1024]{0,1:T(8,128)} %bitcast.80) | data formatting | bytes 1048576
  127.8 6.8 %all-to-all-done.1 = f32[8,16,576]{2,1,0:T(8,128)} async-done(((f32[8,16,576]{2,1,0:T(8,128)}), f32[8,16,576]{2,1,0:T(8,128)}, u32[]{:S(2)}, u32[]{:S(2)}) %all-to-all-start.1) | async-done | bytes 294944 | tf_op jit(solution)/shard_map/all_to_all | solution.py:43
  134.6 1.6 %reduce_sum.29 = f32[16,576]{1,0:T(8,128)} reduce(f32[8,16,576]{2,1,0:T(8,128)} %all-to-all-done.1, f32[]{:T(128)} %constant.21.clone.1), dimensions={0}, to_apply=%region_3.4 | reduce | flops 64512 | bytes 331780 | tf_op jit(solution)/shard_map/reduce_sum | solution.py:44
  (43 shorter events, 14.6 us)
Async XLA Ops:
  0.6 52.9 %copy-start = (bf16[512,1024]{1,0:T(8,128)(2,1)S(1)}, bf16[512,1024]{1,0:T(8,128)(2,1)}, u32[]{:S(2)}) copy-start(bf16[512,1024]{1,0:T(8,128)(2,1)} %param.11) | copy-start | bytes 3145732
  2.1 17.2 %all-to-all-start = ((bf16[8,16,576]{2,1,0:T(8,128)(2,1)}), bf16[8,16,576]{2,1,0:T(8,128)(2,1)S(1)}, u32[]{:S(2)}, u32[]{:S(2)}) async-start(bf16[8,16,576]{2,1,0:T(8,128)(2,1)} %broadcast_in_dim.19), calls=%async_computation | async-start | bytes 327680 | tf_op jit(solution)/shard_map/all_to_all | solution.py:22
  19.5 20.0 %collective-permute-start.2 = (bf16[128,576]{0,1:T(8,128)(2,1)S(1)}, bf16[128,576]{0,1:T(8,128)(2,1)S(1)}, u32[]{:S(2)}, u32[]{:S(2)}) collective-permute-start(bf16[128,576]{0,1:T(8,128)(2,1)S(1)} %copy.29), channel_id=1, source_target_pairs={{0,8},{8,16},{16,24},{24,32},{32,40},{40,48},{48,56},{56,64},{64,7... | collective-permute-start | bytes 442376 | tf_op jit(solution)/shard_map/ppermute | solution.py:32
  31.4 8.2 %collective-permute-start.1 = (bf16[128,576]{0,1:T(8,128)(2,1)S(1)}, bf16[128,576]{0,1:T(8,128)(2,1)S(1)}, u32[]{:S(2)}, u32[]{:S(2)}) collective-permute-start(bf16[128,576]{0,1:T(8,128)(2,1)S(1)} %copy.29), channel_id=1, source_target_pairs={{0,16},{8,24},{16,32},{24,40},{32,48},{40,56},{48,64},{56,72},{64,... | collective-permute-start | bytes 442376 | tf_op jit(solution)/shard_map/ppermute | solution.py:32
  35.0 14.3 %collective-permute-start = (bf16[128,576]{0,1:T(8,128)(2,1)S(1)}, bf16[128,576]{0,1:T(8,128)(2,1)S(1)}, u32[]{:S(2)}, u32[]{:S(2)}) collective-permute-start(bf16[128,576]{0,1:T(8,128)(2,1)S(1)} %copy.29), channel_id=1, source_target_pairs={{0,24},{8,32},{16,40},{24,48},{32,56},{40,64},{48,72},{56,80},{64,... | collective-permute-start | bytes 442376 | tf_op jit(solution)/shard_map/ppermute | solution.py:32
  49.4 0.8 copy-start.7
  58.3 0.6 copy-start.5
  58.9 2.0 %copy-start.1 = (f32[8,128,512]{1,2,0:T(8,128)}, f32[8,128,512]{1,2,0:T(8,128)S(1)}, u32[]{:S(2)}) copy-start(f32[8,128,512]{1,2,0:T(8,128)S(1)} %fusion.4) | copy-start | bytes 6291460
  60.8 4.2 %copy-start.2 = (bf16[512,1024]{0,1:T(8,128)(2,1)S(1)}, bf16[512,1024]{0,1:T(8,128)(2,1)}, u32[]{:S(2)}) copy-start(bf16[512,1024]{0,1:T(8,128)(2,1)} %copy.60) | copy-start | bytes 3145732
  71.6 1.2 copy-start.3
  71.6 1.5 %copy-start.4 = (bf16[8,512,128]{1,2,0:T(8,128)(2,1)S(1)}, bf16[8,512,128]{1,2,0:T(8,128)(2,1)}, u32[]{:S(2)}) copy-start(bf16[8,512,128]{1,2,0:T(8,128)(2,1)} %convolution_convert_fusion) | copy-start | bytes 3145732
  73.9 29.9 %collective-permute-start.5 = (f32[128,576]{0,1:T(8,128)S(1)}, f32[128,576]{0,1:T(8,128)S(1)}, u32[]{:S(2)}, u32[]{:S(2)}) collective-permute-start(f32[128,576]{0,1:T(8,128)S(1)} %get-tuple-element.9), channel_id=1, source_target_pairs={{8,0},{16,8},{24,16},{32,24},{40,32},{48,40},{56,48},{64,56},{72,6... | collective-permute-start | bytes 884744 | tf_op jit(solution)/shard_map/ppermute | solution.py:32
  76.6 27.3 %collective-permute-start.3 = (f32[128,576]{0,1:T(8,128)S(1)}, f32[128,576]{0,1:T(8,128)S(1)}, u32[]{:S(2)}, u32[]{:S(2)}) collective-permute-start(f32[128,576]{0,1:T(8,128)S(1)} %get-tuple-element.10), channel_id=1, source_target_pairs={{24,0},{32,8},{40,16},{48,24},{56,32},{64,40},{72,48},{80,56},{88,... | collective-permute-start | bytes 884744 | tf_op jit(solution)/shard_map/ppermute | solution.py:32
  87.6 29.0 %collective-permute-start.4 = (f32[128,576]{0,1:T(8,128)S(1)}, f32[128,576]{0,1:T(8,128)S(1)}, u32[]{:S(2)}, u32[]{:S(2)}) collective-permute-start(f32[128,576]{0,1:T(8,128)S(1)} %get-tuple-element.11), channel_id=1, source_target_pairs={{16,0},{24,8},{32,16},{40,24},{48,32},{56,40},{64,48},{72,56},{80,... | collective-permute-start | bytes 884744 | tf_op jit(solution)/shard_map/ppermute | solution.py:32
  119.3 7.5 %copy-start.6 = (bf16[512,64,1]{0,1,2:T(8,128)(2,1)S(1)}, bf16[512,64,1]{0,1,2:T(8,128)(2,1)}, u32[]{:S(2)}) copy-start(bf16[512,64,1]{0,1,2:T(8,128)(2,1)} %copy-done.5) | copy-start | bytes 196612
  119.3 15.3 %all-to-all-start.1 = ((f32[8,16,576]{2,1,0:T(8,128)}), f32[8,16,576]{2,1,0:T(8,128)}, u32[]{:S(2)}, u32[]{:S(2)}) async-start(f32[8,16,576]{2,1,0:T(8,128)} %bitcast.81), calls=%async_computation.1 | async-start | bytes 655360 | tf_op jit(solution)/shard_map/all_to_all | solution.py:43
where the time goes:
time: 137 us; the launch traced here: 136 us
  starting transfers between devices  50.4 us (37%)
  waiting for transfers between devices  45 us (33%)
  matrix products  19.3 us (14%)
  local copies, waits for them, and re-layouts  15.8 us (12%)
  other arithmetic  4.85 us (4%)
    ppermute x6, starting transfers between devices, shifted(): return lax.ppermute(block, axis, route)  36.3 us
    ppermute x6, waiting for transfers between devices, shifted(): return lax.ppermute(block, axis, route)  35.9 us
    all_to_all x1, starting transfers between devices, from_everyone(): return lax.all_to_all(copies, axis, split_axis=0, concat_axis=0, tiled=True)  9.99 us
    unnamed x20, local copies, waits for them, and re-layouts  7.48 us
    all_to_all x1, waiting for transfers between devices, summed_on_arrival(): lax.all_to_all(in_blocks(array, dim, length), axis, 0, 0, tiled=True)  6.76 us
    all_to_all x1, starting transfers between devices, summed_on_arrival(): lax.all_to_all(in_blocks(array, dim, length), axis, 0, 0, tiled=True)  4.19 us
    dot_general x1, matrix products, block_grads(): jnp.einsum('hck,chd->khd', weights, out_heads, preferred_element_type=jnp...  4.15 us
    dot_general x1, matrix products, block_grads(): jnp.einsum('hck,khd->chd', weights, value_heads, preferred_element_type=j...  3.1 us
  transfers between devices with their start and end apart: 8, of which 5 were waited for; matrix products, arithmetic and copies ran while one was open for 7% of the time, Pallas kernels for 0%

commit v1 on v0

v1 whole, which is shorter than its diff:
```python
import math

import jax
import jax.numpy as jnp
import numpy as np
from jax import lax
from jax.experimental import pallas as pl
from jax.experimental.pallas import tpu as pltpu
from jax.sharding import Mesh, PartitionSpec as P

NOPE = 128
ROPE = 64
VDIM = 128
RANK = 512
WIDTH = RANK + ROPE
SCALE = 1.0 / math.sqrt(NOPE + ROPE)
LOG2E = 1.4426950408889634
BF16 = jnp.bfloat16
F32 = jnp.float32
NT = (((1,), (1,)), ((), ()))
TN = (((0,), (0,)), ((), ()))
VMEM = pl.BlockSpec(memory_space=pltpu.VMEM)
SMEM = pl.BlockSpec(memory_space=pltpu.SMEM)
PARAMS = pltpu.CompilerParams(vmem_limit_bytes=48 * 1024 * 1024)


def dot(a, b, dims=(((1,), (0,)), ((), ()))):
    return lax.dot_general(a, b, dims, preferred_element_type=F32)


def absorb_kernel(where_ref, keep_ref, qn_ref, qr_ref, go_ref, kup_ref, vup_ref, ql_ref, g_ref, bias_ref):
    heads = kup_ref.shape[1] // NOPE
    group = qn_ref.shape[0]
    for h in range(heads):
        rows = pl.ds(h * group, group)
        cols = pl.ds(h * NOPE, NOPE)
        ql_ref[rows, :RANK] = dot(qn_ref[:, cols], kup_ref[:, cols], NT).astype(BF16)
        ql_ref[rows, RANK:] = qr_ref[:, pl.ds(h * ROPE, ROPE)]
        g_ref[rows, :] = dot(go_ref[:, cols], vup_ref[:, cols], NT).astype(BF16)
    col, hi, core = where_ref[0], where_ref[1], where_ref[2]
    position = 2 * col + hi
    row = lax.broadcasted_iota(jnp.int32, bias_ref.shape, 0)
    query = lax.broadcasted_iota(jnp.int32, bias_ref.shape, 1)
    low = row & 15
    slot = (row >> 4) & 1
    lo = (row >> 5) & 3
    source = (row >> 7) & 1
    side = (row >> 8) ^ core
    back_even = jnp.where(slot == 0, 3 * source, 2 - source)
    back_odd = jnp.where(slot == 0, 1 - source, 3 - source)
    back = jnp.where(hi == 0, back_even, back_odd)
    token = (lo * 2 + side) * 16 + low
    kept = jnp.where(
        back == 1, keep_ref[0, 0], jnp.where(back == 2, keep_ref[0, 1], keep_ref[0, 2])
    )
    seen = jnp.where(
        back == 0,
        (token <= query).astype(jnp.int32),
        ((kept == 1) & (position >= back)).astype(jnp.int32),
    )
    bias_ref[...] = jnp.where(seen == 1, 0.0, -jnp.inf)


def attend_kernel(mine_ref, mate_ref, ql_ref, g_ref, bias_ref, send_ref, ds_ref, wt_ref, lat_ref):
    half = mine_ref.shape[0]
    group = bias_ref.shape[1]
    pairs = ql_ref.shape[0] // (2 * group)
    lat_ref[:half] = mine_ref[...]
    lat_ref[half:] = mate_ref[...]
    for pair in range(pairs):
        cols = pl.ds(pair * 2 * group, 2 * group)
        bias = bias_ref[...]
        bias = jnp.concatenate([bias, bias], axis=1)
        scores = dot(lat_ref[...], ql_ref[cols, :], NT) * (SCALE * LOG2E) + bias
        top = jnp.max(scores, axis=0, keepdims=True)
        exponent = jnp.exp2(scores - top)
        probs = exponent * (1.0 / jnp.sum(exponent, axis=0, keepdims=True))
        weights = probs.astype(BF16)
        wt_ref[:, cols] = weights
        slopes = dot(lat_ref[:, :RANK], g_ref[cols, :], NT)
        delta = jnp.sum(weights.astype(F32) * slopes, axis=0, keepdims=True)
        ds_ref[:, cols] = (probs * ((slopes - delta) * SCALE)).astype(BF16)
    content = dot(ds_ref[half:, :], ql_ref[:, :RANK]) + dot(wt_ref[half:, :], g_ref[...])
    send_ref[:, :RANK] = content.astype(BF16)
    send_ref[:, RANK:] = dot(ds_ref[half:, :], ql_ref[:, RANK:]).astype(BF16)


def own_kernel(ds_ref, wt_ref, ql_ref, g_ref, own_ref):
    half = own_ref.shape[0]
    content = dot(ds_ref[:half, :], ql_ref[:, :RANK]) + dot(wt_ref[:half, :], g_ref[...])
    own_ref[:, :RANK] = content
    own_ref[:, RANK:] = dot(ds_ref[:half, :], ql_ref[:, RANK:])


def query_kernel(mine_ref, mate_ref, ds_ref, kup_ref, dqn_ref, dqr_ref):
    half = mine_ref.shape[0]
    group = dqn_ref.shape[0]
    heads = kup_ref.shape[1] // NOPE
    for h in range(heads):
        cols = pl.ds(h * group, group)
        absorbed = dot(ds_ref[:half, cols], mine_ref[...], TN) + dot(ds_ref[half:, cols], mate_ref[...], TN)
        nope = pl.ds(h * NOPE, NOPE)
        dqn_ref[:, nope] = dot(absorbed[:, :RANK].astype(BF16), kup_ref[:, nope])
        dqr_ref[:, pl.ds(h * ROPE, ROPE)] = absorbed[:, RANK:]


def call(kernel, outs, specs, scratch=(), flops=0, nbytes=0):
    return pl.pallas_call(
        kernel,
        out_shape=[jax.ShapeDtypeStruct(s, t) for s, t in outs],
        in_specs=specs,
        out_specs=[VMEM] * len(outs),
        scratch_shapes=scratch,
        compiler_params=PARAMS,
        cost_estimate=pl.CostEstimate(flops=flops, bytes_accessed=nbytes, transcendentals=0),
    )


def on_device(query_nope, query_rope, grad_out, latent, key_up, value_up, block_keep):
    group = query_nope.shape[0]
    rows, width = latent.shape
    heads = key_up.shape[1] // NOPE
    columns = lax.axis_size("col")
    chips = lax.axis_size("hi") * lax.axis_size("lo")
    chips_lo = lax.axis_size("lo")
    total = heads * group
    window = 4 * group
    half = window // 2
    hi = lax.axis_index("hi")
    where = jnp.stack([lax.axis_index("col"), hi, lax.axis_index("core")]).astype(jnp.int32)

    back1 = lax.ppermute(latent, "col", [(i, i + 1) for i in range(columns - 1)])
    back2 = lax.ppermute(latent, ("col", "hi"), [(2 * i + 1, 2 * i + 5) for i in range(columns - 2)])

    ql, g, bias = call(
        absorb_kernel,
        [((total, width), BF16), ((total, RANK), BF16), ((window, group), F32)],
        [SMEM, SMEM] + [VMEM] * 5,
        flops=4 * total * NOPE * RANK,
        nbytes=5 << 20,
    )(where, block_keep, query_nope, query_rope, grad_out, key_up, value_up)

    to_even = jnp.concatenate([jnp.where(hi == 1, back2, latent), back1], axis=0)
    to_odd = jnp.concatenate([latent, back1], axis=0)
    pieces = jnp.concatenate(
        [jnp.broadcast_to(p, (chips_lo, 2 * rows, width)) for p in (to_even, to_odd)], axis=0
    )
    mine = lax.all_to_all(pieces, ("hi", "lo"), 0, 0, tiled=True).reshape(half, width)
    swap = [(0, 1), (1, 0)]
    mate = lax.ppermute(mine, "core", swap)

    send, ds, wt = call(
        attend_kernel,
        [((half, width), BF16), ((window, total), BF16), ((window, total), BF16)],
        [VMEM] * 5,
        scratch=[pltpu.VMEM((window, width), BF16)],
        flops=6 * total * window * width,
        nbytes=5 << 20,
    )(mine, mate, ql, g, bias)
    arrived = lax.ppermute(send, "core", swap)
    (own,) = call(
        own_kernel,
        [((half, width), F32)],
        [VMEM] * 4,
        flops=4 * half * total * width,
        nbytes=4 << 20,
    )(ds, wt, ql, g)
    summed = (own + arrived.astype(F32)).astype(BF16).reshape(chips, 2 * rows, width)
    parts = lax.all_to_all(summed, ("hi", "lo"), 0, 0, tiled=True)
    d_nope, d_rope = call(
        query_kernel,
        [((group, heads * NOPE), F32), ((group, heads * ROPE), F32)],
        [VMEM] * 4,
        flops=2 * total * window * width + 2 * total * RANK * NOPE,
        nbytes=4 << 20,
    )(mine, mate, ds, key_up)
    parts = parts.reshape(2, chips_lo, 2, rows, width).astype(F32)
    sums = jnp.sum(parts, axis=1)
    from_even = sums[0, 0]
    local = sums[1, 0] + jnp.where(hi == 0, from_even, 0.0)
    to_back1 = (sums[0, 1] + sums[1, 1]).astype(BF16)
    to_back2 = from_even.astype(BF16)
    came1 = lax.ppermute(to_back1, "col", [(i + 1, i) for i in range(columns - 1)])
    came2 = lax.ppermute(to_back2, ("col", "hi"), [(2 * i + 5, 2 * i + 1) for i in range(columns - 2)])
    d_latent = local + came1.astype(F32) + came2.astype(F32)
    return (d_nope, d_rope, d_latent)


def solution(mesh):
    fine = Mesh(mesh.devices.reshape(-1, 2, 4, 2), ("col", "hi", "lo", "core"))
    ctx, head = ("col", "hi"), ("lo", "core")
    placed = (
        P(ctx, head),
        P(ctx, head),
        P(ctx, head),
        P((*ctx, *head), None),
        P(None, head),
        P(None, head),
        P(ctx, None),
    )
    return jax.shard_map(
        on_device,
        mesh=fine,
        in_specs=placed,
        out_specs=(P(ctx, head), P(ctx, head), P((*ctx, *head), None)),
        check_vma=False,
    )
```

time: 137 us -> 81.6 us (0.60)
  the two profiles are of different devices: /device:TPU:40 before, /device:TPU:8 now
where the time goes in v1:
time: 81.6 us; the launch traced here: 81.1 us
  blocking collectives  32.4 us (40%)
  waiting for transfers between devices  19.8 us (24%)
  starting transfers between devices  15 us (18%)
  Pallas kernels  8.64 us (11%)
  other arithmetic  3.1 us (4%)
  local copies, waits for them, and re-layouts  1.28 us (2%)
  between operations  0.85 us (1%)
    all_to_all x1, blocking collectives, on_device(): lax.all_to_all(pieces, ('hi', 'lo'), 0, 0, tiled=True).reshape(half, width)  32.4 us
    all_to_all x1, waiting for transfers between devices, on_device(): parts = lax.all_to_all(summed, ('hi', 'lo'), 0, 0, tiled=True)  14 us
    ppermute x1, waiting for transfers between devices, on_device(): lax.ppermute(latent, 'col', [(i, i + 1) for i in range(columns - 1)])  4.82 us
    ppermute x1, starting transfers between devices, on_device(): lax.ppermute(latent, 'col', [(i, i + 1) for i in range(columns - 1)])  3.6 us
    all_to_all x1, starting transfers between devices, on_device(): parts = lax.all_to_all(summed, ('hi', 'lo'), 0, 0, tiled=True)  3.43 us
    pallas_call x1, Pallas kernels, on_device(): call(attend_kernel, [((half, width), BF16), ((window, total), BF16), ((wi...  3.28 us
    pallas_call x1, Pallas kernels, on_device(): call(query_kernel, [((group, heads * NOPE), F32), ((group, heads * ROPE),...  2.83 us
    ppermute x1, starting transfers between devices, on_device(): arrived = lax.ppermute(send, 'core', swap)  2.4 us
  transfers between devices with their start and end apart: 7, of which 4 were waited for; matrix products, arithmetic and copies ran while one was open for 1% of the time, Pallas kernels for 7%

profile of v1, /device:TPU:8, one launch (start us, length us, event | category | flops | bytes accessed | tf_op | source)
XLA Modules:
  0.0 81.1 jit_solution(7814302943437669792)
XLA Ops:
  0.7 0.8 collective-permute-start
  1.5 3.6 %collective-permute-start.1 = (bf16[16,576]{1,0:T(8,128)(2,1)}, bf16[16,576]{1,0:T(8,128)(2,1)S(1)}, u32[]{:S(2)}, u32[]{:S(2)}) collective-permute-start(bf16[16,576]{1,0:T(8,128)(2,1)} %param.10), channel_id=1, source_target_pairs={{0,16},{16,32},{32,48},{48,64},{64,80},{80,96},{96,112},{112,128},... | collective-permute-start | bytes 55304 | tf_op jit(solution)/shard_map/ppermute | solution.py:132
  5.1 0.8 broadcast_select_fusion
  5.9 4.8 %collective-permute-done.1 = bf16[16,576]{1,0:T(8,128)(2,1)S(1)} collective-permute-done((bf16[16,576]{1,0:T(8,128)(2,1)}, bf16[16,576]{1,0:T(8,128)(2,1)S(1)}, u32[]{:S(2)}, u32[]{:S(2)}) %collective-permute-start.1) | collective-permute-done | bytes 18464 | tf_op jit(solution)/shard_map/ppermute | solution.py:132
  10.7 0.7 pad_maximum_fusion.2
  11.5 0.1 pad_maximum_fusion
  11.5 32.4 %all_to_all.10 = bf16[8,32,576]{2,1,0:T(8,128)(2,1)S(1)} all-to-all(bf16[8,32,576]{2,1,0:T(8,128)(2,1)S(1)} %pad_maximum_fusion), channel_id=1, replica_groups=mesh['col'=64,'hi'=2,'lo'=4,'core'=2] {'hi','lo'}, dimensions={0} | all-to-all | bytes 589824 | tf_op jit(solution)/shard_map/all_to_all | solution.py:148
  43.9 1.9 %collective-permute-start.2 = (bf16[256,576]{1,0:T(8,128)(2,1)S(1)}, bf16[256,576]{1,0:T(8,128)(2,1)S(1)}, u32[]{:S(2)}, u32[]{:S(2)}) collective-permute-start(bf16[256,576]{1,0:T(8,128)(2,1)S(1)} %bitcast.17), channel_id=1, source_target_pairs={{0,1},{1,0},{2,3},{3,2},{4,5},{5,4},{6,7},{7,6},{8,9},{9,8},{10,11... | collective-permute-start | bytes 884744 | tf_op jit(solution)/shard_map/ppermute | solution.py:150
  45.8 0.1 pad_add_fusion.where_ref
  46.0 0.0 copy-start.1
  46.0 1.2 %copy-done.1 = bf16[512,1024]{1,0:T(8,128)(2,1)S(1)} copy-done((bf16[512,1024]{1,0:T(8,128)(2,1)S(1)}, bf16[512,1024]{1,0:T(8,128)(2,1)}, u32[]{:S(2)}) %copy-start.1) | copy-done | bytes 1048600
  47.2 1.7 %shard_map.94 = (bf16[1024,576]{1,0:T(8,128)(2,1)S(1)}, bf16[1024,512]{1,0:T(8,128)(2,1)S(1)}, f32[512,128]{1,0:T(8,128)S(1)}) custom-call(s32[3]{0:T(128)S(1)} %pad_add_fusion.where_ref, s32[1,3]{1,0:T(1,128)S(1)} %copy-done.5, bf16[128,1024]{1,0:T(8,128)(2,1)S(1)} %copy-done.2, bf16[128,512]{1,0:T(8,128)(2,1)S(1)} %copy-done.4, ...), custom_call_target="tpu_custom_call" | custom-call | flops 268435456 | bytes 5242880 | tf_op jit(solution)/shard_map/pallas_call | solution.py:135
  48.9 3.3 %shard_map.95 = (bf16[256,576]{1,0:T(8,128)(2,1)S(1)}, bf16[512,1024]{1,0:T(8,128)(2,1)S(1)}, bf16[512,1024]{1,0:T(8,128)(2,1)S(1)}) custom-call(bf16[256,576]{1,0:T(8,128)(2,1)S(1)} %bitcast.18, bf16[256,576]{1,0:T(8,128)(2,1)S(1)} %collective-permute-done.2.mate_ref, bf16[1024,576]{1,0:T(8,128)(2,1)S(1)} %get-tuple-element.11.ql_ref, ...), custom_call_target="tpu_custom_call" | custom-call | flops 1811939328 | bytes 5242880 | tf_op jit(solution)/shard_map/pallas_call | solution.py:152
  52.2 2.4 %collective-permute-start.3 = (bf16[256,576]{1,0:T(8,128)(2,1)S(1)}, bf16[256,576]{1,0:T(8,128)(2,1)S(1)}, u32[]{:S(2)}, u32[]{:S(2)}) collective-permute-start(bf16[256,576]{1,0:T(8,128)(2,1)S(1)} %get-tuple-element.18), channel_id=1, source_target_pairs={{0,1},{1,0},{2,3},{3,2},{4,5},{5,4},{6,7},{7,6},{8,9},{9,8},{10,11... | collective-permute-start | bytes 884744 | tf_op jit(solution)/shard_map/ppermute | solution.py:160
  54.6 0.8 %shard_map.97 = f32[256,576]{1,0:T(8,128)S(1)} custom-call(bf16[512,1024]{1,0:T(8,128)(2,1)S(1)} %get-tuple-element.14.ds_ref, bf16[512,1024]{1,0:T(8,128)(2,1)S(1)} %get-tuple-element.17.wt_ref, bf16[1024,576]{1,0:T(8,128)(2,1)S(1)} %get-tuple-element.11.ql_ref, bf16[1024,512]{1,0:T(8,128)(2,1)S(1)} %get-tuple-element.12.g_ref), custom_call_target="tpu_custom_call" | custom-call | flops 603979776 | bytes 4194304 | tf_op jit(solution)/shard_map/pallas_call | solution.py:161
  55.4 0.4 collective-permute-done.3
  55.8 0.8 add_convert_fusion
  56.6 3.4 %all-to-all-start.1 = ((bf16[8,32,576]{2,1,0:T(8,128)(2,1)}), bf16[8,32,576]{2,1,0:T(8,128)(2,1)S(1)}, u32[]{:S(2)}, u32[]{:S(2)}) async-start(bf16[8,32,576]{2,1,0:T(8,128)(2,1)} %bitcast.4), calls=%async_computation.1 | async-start | bytes 655360 | tf_op jit(solution)/shard_map/all_to_all | solution.py:169
  60.0 14.0 %all-to-all-done.1 = bf16[8,32,576]{2,1,0:T(8,128)(2,1)S(1)} async-done(((bf16[8,32,576]{2,1,0:T(8,128)(2,1)}), bf16[8,32,576]{2,1,0:T(8,128)(2,1)S(1)}, u32[]{:S(2)}, u32[]{:S(2)}) %all-to-all-start.1) | async-done | bytes 294944 | tf_op jit(solution)/shard_map/all_to_all | solution.py:169
  74.1 0.7 collective-permute-start.5
  74.8 2.2 %collective-permute-start.4 = (bf16[16,576]{1,0:T(8,128)(2,1)S(1)}, bf16[16,576]{1,0:T(8,128)(2,1)S(1)}, u32[]{:S(2)}, u32[]{:S(2)}) collective-permute-start(bf16[16,576]{1,0:T(8,128)(2,1)S(1)} %fusion.5), channel_id=1, source_target_pairs={{16,0},{32,16},{48,32},{64,48},{80,64},{96,80},{112,96},{128,112},... | collective-permute-start | bytes 55304 | tf_op jit(solution)/shard_map/ppermute | solution.py:183
  77.1 2.8 %shard_map.96 = (f32[128,1024]{1,0:T(8,128)}, f32[128,512]{1,0:T(8,128)}) custom-call(bf16[256,576]{1,0:T(8,128)(2,1)S(1)} %bitcast.19, bf16[256,576]{1,0:T(8,128)(2,1)S(1)} %collective-permute-done.2.mate_ref, bf16[512,1024]{1,0:T(8,128)(2,1)S(1)} %get-tuple-element.14.ds_ref, bf16[512,1024]{1,0:T(8,128)(2,1)S(1)} %copy-done), custom_call_target="tpu_custom_call" | custom-call | flops 738197504 | bytes 4194304 | tf_op jit(solution)/shard_map/pallas_call | solution.py:170
  79.9 0.6 collective-permute-done.4
  80.5 0.6 fusion.3
  (18 shorter events, 0.1 us)
Async XLA Ops:
  0.6 45.3 %copy-start = (bf16[512,1024]{1,0:T(8,128)(2,1)S(1)}, bf16[512,1024]{1,0:T(8,128)(2,1)}, u32[]{:S(2)}) copy-start(bf16[512,1024]{1,0:T(8,128)(2,1)} %kup_ref.3) | copy-start | bytes 3145732
  0.6 45.3 %copy-start.5 = (s32[1,3]{1,0:T(1,128)S(1)}, s32[1,3]{1,0:T(1,128)}, u32[]{:S(2)}) copy-start(s32[1,3]{1,0:T(1,128)} %keep_ref.1) | copy-start | bytes 40
  0.7 45.3 %copy-start.3 = (bf16[128,1024]{1,0:T(8,128)(2,1)S(1)}, bf16[128,1024]{1,0:T(8,128)(2,1)}, u32[]{:S(2)}) copy-start(bf16[128,1024]{1,0:T(8,128)(2,1)} %go_ref.1) | copy-start | bytes 786436
  0.7 45.3 %copy-start.4 = (bf16[128,512]{1,0:T(8,128)(2,1)S(1)}, bf16[128,512]{1,0:T(8,128)(2,1)}, u32[]{:S(2)}) copy-start(bf16[128,512]{1,0:T(8,128)(2,1)} %qr_ref.1) | copy-start | bytes 393220
  0.7 45.3 %copy-start.2 = (bf16[128,1024]{1,0:T(8,128)(2,1)S(1)}, bf16[128,1024]{1,0:T(8,128)(2,1)}, u32[]{:S(2)}) copy-start(bf16[128,1024]{1,0:T(8,128)(2,1)} %qn_ref.1) | copy-start | bytes 786436
  0.7 4.4 %collective-permute-start = (bf16[16,576]{1,0:T(8,128)(2,1)}, bf16[16,576]{1,0:T(8,128)(2,1)S(1)}, u32[]{:S(2)}, u32[]{:S(2)}) collective-permute-start(bf16[16,576]{1,0:T(8,128)(2,1)} %param.10), channel_id=1, source_target_pairs={{8,40},{24,56},{40,72},{56,88},{72,104},{88,120},{104,136},{120,15... | collective-permute-start | bytes 55304 | tf_op jit(solution)/shard_map/ppermute | solution.py:133
  1.5 9.2 %collective-permute-start.1 = (bf16[16,576]{1,0:T(8,128)(2,1)}, bf16[16,576]{1,0:T(8,128)(2,1)S(1)}, u32[]{:S(2)}, u32[]{:S(2)}) collective-permute-start(bf16[16,576]{1,0:T(8,128)(2,1)} %param.10), channel_id=1, source_target_pairs={{0,16},{16,32},{32,48},{48,64},{64,80},{80,96},{96,112},{112,128},... | collective-permute-start | bytes 55304 | tf_op jit(solution)/shard_map/ppermute | solution.py:132
  43.9 5.0 %collective-permute-start.2 = (bf16[256,576]{1,0:T(8,128)(2,1)S(1)}, bf16[256,576]{1,0:T(8,128)(2,1)S(1)}, u32[]{:S(2)}, u32[]{:S(2)}) collective-permute-start(bf16[256,576]{1,0:T(8,128)(2,1)S(1)} %bitcast.17), channel_id=1, source_target_pairs={{0,1},{1,0},{2,3},{3,2},{4,5},{5,4},{6,7},{7,6},{8,9},{9,8},{10,11... | collective-permute-start | bytes 884744 | tf_op jit(solution)/shard_map/ppermute | solution.py:150
  46.0 1.2 %copy-start.1 = (bf16[512,1024]{1,0:T(8,128)(2,1)S(1)}, bf16[512,1024]{1,0:T(8,128)(2,1)}, u32[]{:S(2)}) copy-start(bf16[512,1024]{1,0:T(8,128)(2,1)} %vup_ref.1) | copy-start | bytes 3145732
  52.2 3.6 %collective-permute-start.3 = (bf16[256,576]{1,0:T(8,128)(2,1)S(1)}, bf16[256,576]{1,0:T(8,128)(2,1)S(1)}, u32[]{:S(2)}, u32[]{:S(2)}) collective-permute-start(bf16[256,576]{1,0:T(8,128)(2,1)S(1)} %get-tuple-element.18), channel_id=1, source_target_pairs={{0,1},{1,0},{2,3},{3,2},{4,5},{5,4},{6,7},{7,6},{8,9},{9,8},{10,11... | collective-permute-start | bytes 884744 | tf_op jit(solution)/shard_map/ppermute | solution.py:160
  56.6 17.5 %all-to-all-start.1 = ((bf16[8,32,576]{2,1,0:T(8,128)(2,1)}), bf16[8,32,576]{2,1,0:T(8,128)(2,1)S(1)}, u32[]{:S(2)}, u32[]{:S(2)}) async-start(bf16[8,32,576]{2,1,0:T(8,128)(2,1)} %bitcast.4), calls=%async_computation.1 | async-start | bytes 655360 | tf_op jit(solution)/shard_map/all_to_all | solution.py:169
  74.1 5.8 %collective-permute-start.5 = (bf16[16,576]{1,0:T(8,128)(2,1)S(1)}, bf16[16,576]{1,0:T(8,128)(2,1)S(1)}, u32[]{:S(2)}, u32[]{:S(2)}) collective-permute-start(bf16[16,576]{1,0:T(8,128)(2,1)S(1)} %fusion.4), channel_id=1, source_target_pairs={{40,8},{56,24},{72,40},{88,56},{104,72},{120,88},{136,104},{152,12... | collective-permute-start | bytes 55304 | tf_op jit(solution)/shard_map/ppermute | solution.py:184
  74.8 5.7 %collective-permute-start.4 = (bf16[16,576]{1,0:T(8,128)(2,1)S(1)}, bf16[16,576]{1,0:T(8,128)(2,1)S(1)}, u32[]{:S(2)}, u32[]{:S(2)}) collective-permute-start(bf16[16,576]{1,0:T(8,128)(2,1)S(1)} %fusion.5), channel_id=1, source_target_pairs={{16,0},{32,16},{48,32},{64,48},{80,64},{96,80},{112,96},{128,112},... | collective-permute-start | bytes 55304 | tf_op jit(solution)/shard_map/ppermute | solution.py:183

commit v2 on v1

--- a/solution.py
+++ b/solution.py
@@ -15,13 +15,14 @@
 WIDTH = RANK + ROPE
 SCALE = 1.0 / math.sqrt(NOPE + ROPE)
 LOG2E = 1.4426950408889634
+EARLY = 2
 BF16 = jnp.bfloat16
 F32 = jnp.float32
 NT = (((1,), (1,)), ((), ()))
 TN = (((0,), (0,)), ((), ()))
 VMEM = pl.BlockSpec(memory_space=pltpu.VMEM)
 SMEM = pl.BlockSpec(memory_space=pltpu.SMEM)
-PARAMS = pltpu.CompilerParams(vmem_limit_bytes=48 * 1024 * 1024)
+PARAMS = pltpu.CompilerParams(vmem_limit_bytes=16 * 1024 * 1024)
 
 
 def dot(a, b, dims=(((1,), (0,)), ((), ()))):
@@ -61,6 +62,20 @@
     bias_ref[...] = jnp.where(seen == 1, 0.0, -jnp.inf)
 
 
+def stage_kernel(in_ref, out_ref):
+    out_ref[...] = in_ref[...]
+
+
+def pieces_kernel(latent_ref, back1_ref, back2_ref, out_ref):
+    rows = latent_ref.shape[0]
+    chips_lo = out_ref.shape[0] // 2
+    own, back1 = latent_ref[...], back1_ref[...]
+    to_even = jnp.where(lax.axis_index("hi") == 1, back2_ref[...], own)
+    for i in range(2 * chips_lo):
+        out_ref[i, :rows] = to_even if i < chips_lo else own
+        out_ref[i, rows:] = back1
+
+
 def attend_kernel(mine_ref, mate_ref, ql_ref, g_ref, bias_ref, send_ref, ds_ref, wt_ref, lat_ref):
     half = mine_ref.shape[0]
     group = bias_ref.shape[1]
@@ -85,23 +100,45 @@
     send_ref[:, RANK:] = dot(ds_ref[half:, :], ql_ref[:, RANK:]).astype(BF16)
 
 
-def own_kernel(ds_ref, wt_ref, ql_ref, g_ref, own_ref):
-    half = own_ref.shape[0]
-    content = dot(ds_ref[:half, :], ql_ref[:, :RANK]) + dot(wt_ref[:half, :], g_ref[...])
-    own_ref[:, :RANK] = content
-    own_ref[:, RANK:] = dot(ds_ref[:half, :], ql_ref[:, RANK:])
-
-
-def query_kernel(mine_ref, mate_ref, ds_ref, kup_ref, dqn_ref, dqr_ref):
+def query_grads(heads, mine_ref, mate_ref, ds_ref, kup_ref, dqn_ref, dqr_ref):
     half = mine_ref.shape[0]
     group = dqn_ref.shape[0]
-    heads = kup_ref.shape[1] // NOPE
-    for h in range(heads):
+    for h in heads:
         cols = pl.ds(h * group, group)
         absorbed = dot(ds_ref[:half, cols], mine_ref[...], TN) + dot(ds_ref[half:, cols], mate_ref[...], TN)
         nope = pl.ds(h * NOPE, NOPE)
         dqn_ref[:, nope] = dot(absorbed[:, :RANK].astype(BF16), kup_ref[:, nope])
         dqr_ref[:, pl.ds(h * ROPE, ROPE)] = absorbed[:, RANK:]
+
+
+def own_kernel(mine_ref, mate_ref, ds_ref, wt_ref, ql_ref, g_ref, kup_ref, own_ref, dqn_ref, dqr_ref):
+    half = own_ref.shape[0]
+    content = dot(ds_ref[:half, :], ql_ref[:, :RANK]) + dot(wt_ref[:half, :], g_ref[...])
+    own_ref[:, :RANK] = content
+    own_ref[:, RANK:] = dot(ds_ref[:half, :], ql_ref[:, RANK:])
+    query_grads(range(EARLY), mine_ref, mate_ref, ds_ref, kup_ref, dqn_ref, dqr_ref)
+
+
+def add_kernel(own_ref, arrived_ref, sum_ref):
+    sum_ref[...] = (own_ref[...] + arrived_ref[...].astype(F32)).astype(BF16)
+
+
+def query_kernel(mine_ref, mate_ref, ds_ref, kup_ref, early_n_ref, early_r_ref, dqn_ref, dqr_ref):
+    dqn_ref[:, : EARLY * NOPE] = early_n_ref[...]
+    dqr_ref[:, : EARLY * ROPE] = early_r_ref[...]
+    heads = kup_ref.shape[1] // NOPE
+    query_grads(range(EARLY, heads), mine_ref, mate_ref, ds_ref, kup_ref, dqn_ref, dqr_ref)
+
+
+def owners_kernel(parts_ref, local_ref, to_back1_ref, to_back2_ref):
+    chips_lo = parts_ref.shape[0] // 2
+    rows = local_ref.shape[0]
+    even = [parts_ref[i].astype(F32) for i in range(chips_lo)]
+    odd = [parts_ref[chips_lo + i].astype(F32) for i in range(chips_lo)]
+    even, odd = sum(even[1:], even[0]), sum(odd[1:], odd[0])
+    to_back1_ref[...] = (even[rows:] + odd[rows:]).astype(BF16)
+    to_back2_ref[...] = even[:rows].astype(BF16)
+    local_ref[...] = odd[:rows] + jnp.where(lax.axis_index("hi") == 0, even[:rows], 0.0)
 
 
 def call(kernel, outs, specs, scratch=(), flops=0, nbytes=0):
@@ -122,12 +159,10 @@
     heads = key_up.shape[1] // NOPE
     columns = lax.axis_size("col")
     chips = lax.axis_size("hi") * lax.axis_size("lo")
-    chips_lo = lax.axis_size("lo")
     total = heads * group
     window = 4 * group
     half = window // 2
-    hi = lax.axis_index("hi")
-    where = jnp.stack([lax.axis_index("col"), hi, lax.axis_index("core")]).astype(jnp.int32)
+    where = jnp.stack([lax.axis_index(name) for name in ("col", "hi", "core")]).astype(jnp.int32)
 
     back1 = lax.ppermute(latent, "col", [(i, i + 1) for i in range(columns - 1)])
     back2 = lax.ppermute(latent, ("col", "hi"), [(2 * i + 1, 2 * i + 5) for i in range(columns - 2)])
@@ -139,16 +174,17 @@
         flops=4 * total * NOPE * RANK,
         nbytes=5 << 20,
     )(where, block_keep, query_nope, query_rope, grad_out, key_up, value_up)
-
-    to_even = jnp.concatenate([jnp.where(hi == 1, back2, latent), back1], axis=0)
-    to_odd = jnp.concatenate([latent, back1], axis=0)
-    pieces = jnp.concatenate(
-        [jnp.broadcast_to(p, (chips_lo, 2 * rows, width)) for p in (to_even, to_odd)], axis=0
-    )
+    (staged,) = call(stage_kernel, [((rows, width), BF16)], [VMEM], flops=4 << 30, nbytes=4 << 20)(latent)
+    (pieces,) = call(
+        pieces_kernel,
+        [((chips, 2 * rows, width), BF16)],
+        [VMEM] * 3,
+        flops=4 << 30,
+        nbytes=4 << 20,
+    )(staged, back1, back2)
     mine = lax.all_to_all(pieces, ("hi", "lo"), 0, 0, tiled=True).reshape(half, width)
     swap = [(0, 1), (1, 0)]
     mate = lax.ppermute(mine, "core", swap)
-
     send, ds, wt = call(
         attend_kernel,
         [((half, width), BF16), ((window, total), BF16), ((window, total), BF16)],
@@ -158,30 +194,29 @@
         nbytes=5 << 20,
     )(mine, mate, ql, g, bias)
     arrived = lax.ppermute(send, "core", swap)
-    (own,) = call(
+    own, early_n, early_r = call(
         own_kernel,
-        [((half, width), F32)],
-        [VMEM] * 4,
+        [((half, width), F32), ((group, EARLY * NOPE), F32), ((group, EARLY * ROPE), F32)],
+        [VMEM] * 7,
         flops=4 * half * total * width,
         nbytes=4 << 20,
-    )(ds, wt, ql, g)
-    summed = (own + arrived.astype(F32)).astype(BF16).reshape(chips, 2 * rows, width)
-    parts = lax.all_to_all(summed, ("hi", "lo"), 0, 0, tiled=True)
+    )(mine, mate, ds, wt, ql, g, key_up)
+    (summed,) = call(add_kernel, [((half, width), BF16)], [VMEM] * 2)(own, arrived)
+    parts = lax.all_to_all(summed.reshape(chips, 2 * rows, width), ("hi", "lo"), 0, 0, tiled=True)
+    local, to_back1, to_back2 = call(
+        owners_kernel,
+        [((rows, width), F32), ((rows, width), BF16), ((rows, width), BF16)],
+        [VMEM],
+    )(parts)
     d_nope, d_rope = call(
         query_kernel,
         [((group, heads * NOPE), F32), ((group, heads * ROPE), F32)],
-        [VMEM] * 4,
+        [VMEM] * 6,
         flops=2 * total * window * width + 2 * total * RANK * NOPE,
         nbytes=4 << 20,
-    )(mine, mate, ds, key_up)
-    parts = parts.reshape(2, chips_lo, 2, rows, width).astype(F32)
-    sums = jnp.sum(parts, axis=1)
-    from_even = sums[0, 0]
-    local = sums[1, 0] + jnp.where(hi == 0, from_even, 0.0)
-    to_back1 = (sums[0, 1] + sums[1, 1]).astype(BF16)
-    to_back2 = from_even.astype(BF16)
+    )(mine, mate, ds, key_up, early_n, early_r)
+    came2 = lax.ppermute(to_back2, ("col", "hi"), [(2 * i + 5, 2 * i + 1) for i in range(columns - 2)])
     came1 = lax.ppermute(to_back1, "col", [(i + 1, i) for i in range(columns - 1)])
-    came2 = lax.ppermute(to_back2, ("col", "hi"), [(2 * i + 5, 2 * i + 1) for i in range(columns - 2)])
     d_latent = local + came1.astype(F32) + came2.astype(F32)
     return (d_nope, d_rope, d_latent)
 

time: 81.6 us -> 77 us (0.944)
  blocking collectives: 32.4 us -> 48.9 us
  waiting for transfers between devices: 19.8 us -> 5.23 us
  starting transfers between devices: 15 us -> 11.5 us
  other arithmetic: 3.1 us -> 0.7 us
    all_to_all x0 -> x1, blocking collectives: none -> 16.4 us  [on_device(): lax.all_to_all(summed.reshape(chips, 2 * rows, width), ('hi', 'lo'), 0, 0...]
    all_to_all x1 -> x0, waiting for transfers between devices: 14 us -> none  [on_device(): parts = lax.all_to_all(summed, ('hi', 'lo'), 0, 0, tiled=True)]
    all_to_all x1 -> x0, starting transfers between devices: 3.43 us -> none  [on_device(): parts = lax.all_to_all(summed, ('hi', 'lo'), 0, 0, tiled=True)]
  transfers between devices with their start and end apart: 7 -> 6, of which waited for: 4 -> 2; matrix products, arithmetic and copies ran while one was open for 1% -> 0% of each run, Pallas kernels for 7% -> 7%
where the time goes in v2:
time: 77 us; the launch traced here: 76.7 us
  blocking collectives  48.9 us (64%)
  starting transfers between devices  11.5 us (15%)
  Pallas kernels  8.77 us (11%)
  waiting for transfers between devices  5.23 us (7%)
  between operations  0.8 us (1%)
    all_to_all x1, blocking collectives, on_device(): lax.all_to_all(pieces, ('hi', 'lo'), 0, 0, tiled=True).reshape(half, width)  32.5 us
    all_to_all x1, blocking collectives, on_device(): lax.all_to_all(summed.reshape(chips, 2 * rows, width), ('hi', 'lo'), 0, 0...  16.4 us
    ppermute x1, waiting for transfers between devices, on_device(): lax.ppermute(latent, 'col', [(i, i + 1) for i in range(columns - 1)])  4.82 us
    ppermute x1, starting transfers between devices, on_device(): lax.ppermute(latent, 'col', [(i, i + 1) for i in range(columns - 1)])  3.6 us
    pallas_call x1, Pallas kernels, on_device(): call(attend_kernel, [((half, width), BF16), ((window, total), BF16), ((wi...  3.28 us
    ppermute x1, starting transfers between devices, on_device(): arrived = lax.ppermute(send, 'core', swap)  2.41 us
    pallas_call x1, Pallas kernels, on_device(): call(query_kernel, [((group, heads * NOPE), F32), ((group, heads * ROPE),...  2.36 us
    ppermute x1, starting transfers between devices, on_device(): lax.ppermute(to_back1, 'col', [(i + 1, i) for i in range(columns - 1)])  2.24 us
  transfers between devices with their start and end apart: 6, of which 2 were waited for; matrix products, arithmetic and copies ran while one was open for 0% of the time, Pallas kernels for 7%

profile of v2, /device:TPU:8, one launch (start us, length us, event | category | flops | bytes accessed | tf_op | source)
XLA Modules:
  0.0 76.7 jit_solution(8662401497150855151)
XLA Ops:
  0.6 0.7 collective-permute-start.1
  1.3 3.6 %collective-permute-start = (bf16[16,576]{1,0:T(8,128)(2,1)}, bf16[16,576]{1,0:T(8,128)(2,1)S(1)}, u32[]{:S(2)}, u32[]{:S(2)}) collective-permute-start(bf16[16,576]{1,0:T(8,128)(2,1)} %in_ref.1), channel_id=1, source_target_pairs={{0,16},{16,32},{32,48},{48,64},{64,80},{80,96},{96,112},{112,128},... | collective-permute-start | bytes 55304 | tf_op jit(solution)/shard_map/ppermute | solution.py:167
  4.9 0.0 copy-start.6
  4.9 0.7 copy-done.6
  5.7 0.0 copy-start.5
  5.7 0.0 collective-permute-done.1.back2_ref
  5.7 4.8 %collective-permute-done.back1_ref = bf16[16,576]{1,0:T(8,128)(2,1)S(1)} collective-permute-done((bf16[16,576]{1,0:T(8,128)(2,1)}, bf16[16,576]{1,0:T(8,128)(2,1)S(1)}, u32[]{:S(2)}, u32[]{:S(2)}) %collective-permute-start) | collective-permute-done | bytes 18464 | tf_op jit(solution)/shard_map/ppermute | solution.py:167
  10.5 32.5 %all_to_all.10 = bf16[8,32,576]{2,1,0:T(8,128)(2,1)S(1)} all-to-all(bf16[8,32,576]{2,1,0:T(8,128)(2,1)S(1)} %shard_map.95), channel_id=1, replica_groups=mesh['col'=64,'hi'=2,'lo'=4,'core'=2] {'hi','lo'}, dimensions={0} | all-to-all | bytes 589824 | tf_op jit(solution)/shard_map/all_to_all | solution.py:185
  43.1 1.9 %collective-permute-start.2 = (bf16[256,576]{1,0:T(8,128)(2,1)S(1)}, bf16[256,576]{1,0:T(8,128)(2,1)S(1)}, u32[]{:S(2)}, u32[]{:S(2)}) collective-permute-start(bf16[256,576]{1,0:T(8,128)(2,1)S(1)} %bitcast.5), channel_id=1, source_target_pairs={{0,1},{1,0},{2,3},{3,2},{4,5},{5,4},{6,7},{7,6},{8,9},{9,8},{10,11... | collective-permute-start | bytes 884744 | tf_op jit(solution)/shard_map/ppermute | solution.py:187
  45.0 0.1 pad_add_fusion.where_ref
  45.1 1.7 %shard_map.96 = (bf16[1024,576]{1,0:T(8,128)(2,1)S(1)}, bf16[1024,512]{1,0:T(8,128)(2,1)S(1)}, f32[512,128]{1,0:T(8,128)S(1)}) custom-call(s32[3]{0:T(128)S(1)} %pad_add_fusion.where_ref, s32[1,3]{1,0:T(1,128)S(1)} %copy-done.5, bf16[128,1024]{1,0:T(8,128)(2,1)S(1)} %copy-done.2, bf16[128,512]{1,0:T(8,128)(2,1)S(1)} %copy-done.4, ...), custom_call_target="tpu_custom_call" | custom-call | flops 268435456 | bytes 5242880 | tf_op jit(solution)/shard_map/pallas_call | solution.py:170
  46.8 0.0 collective-permute-done.2.mate_ref
  46.8 3.3 %shard_map.97 = (bf16[256,576]{1,0:T(8,128)(2,1)S(1)}, bf16[512,1024]{1,0:T(8,128)(2,1)S(1)}, bf16[512,1024]{1,0:T(8,128)(2,1)S(1)}) custom-call(bf16[256,576]{1,0:T(8,128)(2,1)S(1)} %bitcast.6, bf16[256,576]{1,0:T(8,128)(2,1)S(1)} %collective-permute-done.2.mate_ref, bf16[1024,576]{1,0:T(8,128)(2,1)S(1)} %get-tuple-element.17.ql_ref, ...), custom_call_target="tpu_custom_call" | custom-call | flops 1811939328 | bytes 5242880 | tf_op jit(solution)/shard_map/pallas_call | solution.py:188
  50.1 2.4 %collective-permute-start.3 = (bf16[256,576]{1,0:T(8,128)(2,1)S(1)}, bf16[256,576]{1,0:T(8,128)(2,1)S(1)}, u32[]{:S(2)}, u32[]{:S(2)}) collective-permute-start(bf16[256,576]{1,0:T(8,128)(2,1)S(1)} %get-tuple-element.27), channel_id=1, source_target_pairs={{0,1},{1,0},{2,3},{3,2},{4,5},{5,4},{6,7},{7,6},{8,9},{9,8},{10,11... | collective-permute-start | bytes 884744 | tf_op jit(solution)/shard_map/ppermute | solution.py:196
  52.5 1.3 %shard_map.98 = (f32[256,576]{1,0:T(8,128)S(1)}, f32[128,256]{1,0:T(8,128)S(1)}, f32[128,128]{1,0:T(8,128)S(1)}) custom-call(bf16[256,576]{1,0:T(8,128)(2,1)S(1)} %bitcast.7, bf16[256,576]{1,0:T(8,128)(2,1)S(1)} %collective-permute-done.2.mate_ref, bf16[512,1024]{1,0:T(8,128)(2,1)S(1)} %get-tuple-element.20.ds_ref, ...), custom_call_target="tpu_custom_call" | custom-call | flops 603979776 | bytes 4194304 | tf_op jit(solution)/shard_map/pallas_call | solution.py:197
  53.8 0.0 collective-permute-done.3.arrived_ref
  53.8 0.1 shard_map.100
  53.9 16.4 %all_to_all.11.parts_ref = bf16[8,32,576]{2,1,0:T(8,128)(2,1)S(1)} all-to-all(bf16[8,32,576]{2,1,0:T(8,128)(2,1)S(1)} %bitcast.9), channel_id=1, replica_groups=mesh['col'=64,'hi'=2,'lo'=4,'core'=2] {'hi','lo'}, dimensions={0} | all-to-all | bytes 589824 | tf_op jit(solution)/shard_map/all_to_all | solution.py:205
  70.3 2.2 %collective-permute-start.4 = (bf16[16,576]{1,0:T(8,128)(2,1)S(1)}, bf16[16,576]{1,0:T(8,128)(2,1)S(1)}, u32[]{:S(2)}, u32[]{:S(2)}) collective-permute-start(bf16[16,576]{1,0:T(8,128)(2,1)S(1)} %get-tuple-element.29), channel_id=1, source_target_pairs={{16,0},{32,16},{48,32},{64,48},{80,64},{96,80},{112,96},{128,112},... | collective-permute-start | bytes 55304 | tf_op jit(solution)/shard_map/ppermute | solution.py:219
  72.6 0.7 collective-permute-start.5
  73.3 2.4 %shard_map.99 = (f32[128,1024]{1,0:T(8,128)}, f32[128,512]{1,0:T(8,128)}) custom-call(bf16[256,576]{1,0:T(8,128)(2,1)S(1)} %bitcast.8, bf16[256,576]{1,0:T(8,128)(2,1)S(1)} %collective-permute-done.2.mate_ref, bf16[512,1024]{1,0:T(8,128)(2,1)S(1)} %get-tuple-element.20.ds_ref, bf16[512,1024]{1,0:T(8,128)(2,1)S(1)} %copy-done, ...), custom_call_target="tpu_custom_call" | custom-call | flops 738197504 | bytes 4194304 | tf_op jit(solution)/shard_map/pallas_call | solution.py:211
  75.6 0.4 collective-permute-done.4
  76.0 0.0 collective-permute-done.5
  76.0 0.6 convert_add_fusion
  (14 shorter events, 0.1 us)
Async XLA Ops:
  0.6 5.0 %collective-permute-start.1 = (bf16[16,576]{1,0:T(8,128)(2,1)}, bf16[16,576]{1,0:T(8,128)(2,1)S(1)}, u32[]{:S(2)}, u32[]{:S(2)}) collective-permute-start(bf16[16,576]{1,0:T(8,128)(2,1)} %in_ref.1), channel_id=1, source_target_pairs={{8,40},{24,56},{40,72},{56,88},{72,104},{88,120},{104,136},{120,15... | collective-permute-start | bytes 55304 | tf_op jit(solution)/shard_map/ppermute | solution.py:168
  1.3 9.2 %collective-permute-start = (bf16[16,576]{1,0:T(8,128)(2,1)}, bf16[16,576]{1,0:T(8,128)(2,1)S(1)}, u32[]{:S(2)}, u32[]{:S(2)}) collective-permute-start(bf16[16,576]{1,0:T(8,128)(2,1)} %in_ref.1), channel_id=1, source_target_pairs={{0,16},{16,32},{32,48},{48,64},{64,80},{80,96},{96,112},{112,128},... | collective-permute-start | bytes 55304 | tf_op jit(solution)/shard_map/ppermute | solution.py:167
  4.9 0.7 copy-start.6
  5.6 39.4 %copy-start.2 = (bf16[128,1024]{1,0:T(8,128)(2,1)S(1)}, bf16[128,1024]{1,0:T(8,128)(2,1)}, u32[]{:S(2)}) copy-start(bf16[128,1024]{1,0:T(8,128)(2,1)} %qn_ref.1) | copy-start | bytes 786436
  5.7 39.4 %copy-start.3 = (bf16[128,1024]{1,0:T(8,128)(2,1)S(1)}, bf16[128,1024]{1,0:T(8,128)(2,1)}, u32[]{:S(2)}) copy-start(bf16[128,1024]{1,0:T(8,128)(2,1)} %go_ref.1) | copy-start | bytes 786436
  5.7 39.4 %copy-start.4 = (bf16[128,512]{1,0:T(8,128)(2,1)S(1)}, bf16[128,512]{1,0:T(8,128)(2,1)}, u32[]{:S(2)}) copy-start(bf16[128,512]{1,0:T(8,128)(2,1)} %qr_ref.1) | copy-start | bytes 393220
  5.7 39.4 %copy-start.5 = (s32[1,3]{1,0:T(1,128)S(1)}, s32[1,3]{1,0:T(1,128)}, u32[]{:S(2)}) copy-start(s32[1,3]{1,0:T(1,128)} %keep_ref.1) | copy-start | bytes 40
  10.5 34.6 %copy-start = (bf16[512,1024]{1,0:T(8,128)(2,1)S(1)}, bf16[512,1024]{1,0:T(8,128)(2,1)}, u32[]{:S(2)}) copy-start(bf16[512,1024]{1,0:T(8,128)(2,1)} %kup_ref.5) | copy-start | bytes 3145732
  10.5 34.6 %copy-start.1 = (bf16[512,1024]{1,0:T(8,128)(2,1)S(1)}, bf16[512,1024]{1,0:T(8,128)(2,1)}, u32[]{:S(2)}) copy-start(bf16[512,1024]{1,0:T(8,128)(2,1)} %vup_ref.1) | copy-start | bytes 3145732
  43.1 3.7 %collective-permute-start.2 = (bf16[256,576]{1,0:T(8,128)(2,1)S(1)}, bf16[256,576]{1,0:T(8,128)(2,1)S(1)}, u32[]{:S(2)}, u32[]{:S(2)}) collective-permute-start(bf16[256,576]{1,0:T(8,128)(2,1)S(1)} %bitcast.5), channel_id=1, source_target_pairs={{0,1},{1,0},{2,3},{3,2},{4,5},{5,4},{6,7},{7,6},{8,9},{9,8},{10,11... | collective-permute-start | bytes 884744 | tf_op jit(solution)/shard_map/ppermute | solution.py:187
  50.1 3.7 %collective-permute-start.3 = (bf16[256,576]{1,0:T(8,128)(2,1)S(1)}, bf16[256,576]{1,0:T(8,128)(2,1)S(1)}, u32[]{:S(2)}, u32[]{:S(2)}) collective-permute-start(bf16[256,576]{1,0:T(8,128)(2,1)S(1)} %get-tuple-element.27), channel_id=1, source_target_pairs={{0,1},{1,0},{2,3},{3,2},{4,5},{5,4},{6,7},{7,6},{8,9},{9,8},{10,11... | collective-permute-start | bytes 884744 | tf_op jit(solution)/shard_map/ppermute | solution.py:196
  70.3 5.7 %collective-permute-start.4 = (bf16[16,576]{1,0:T(8,128)(2,1)S(1)}, bf16[16,576]{1,0:T(8,128)(2,1)S(1)}, u32[]{:S(2)}, u32[]{:S(2)}) collective-permute-start(bf16[16,576]{1,0:T(8,128)(2,1)S(1)} %get-tuple-element.29), channel_id=1, source_target_pairs={{16,0},{32,16},{48,32},{64,48},{80,64},{96,80},{112,96},{128,112},... | collective-permute-start | bytes 55304 | tf_op jit(solution)/shard_map/ppermute | solution.py:219
  72.6 3.4 %collective-permute-start.5 = (bf16[16,576]{1,0:T(8,128)(2,1)S(1)}, bf16[16,576]{1,0:T(8,128)(2,1)S(1)}, u32[]{:S(2)}, u32[]{:S(2)}) collective-permute-start(bf16[16,576]{1,0:T(8,128)(2,1)S(1)} %get-tuple-element.30), channel_id=1, source_target_pairs={{40,8},{56,24},{72,40},{88,56},{104,72},{120,88},{136,104},{152,12... | collective-permute-start | bytes 55304 | tf_op jit(solution)/shard_map/ppermute | solution.py:218

commit v3 on v2

--- a/solution.py
+++ b/solution.py
@@ -44,8 +44,8 @@
     query = lax.broadcasted_iota(jnp.int32, bias_ref.shape, 1)
     low = row & 15
     slot = (row >> 4) & 1
-    lo = (row >> 5) & 3
-    source = (row >> 7) & 1
+    source = (row >> 5) & 1
+    lo = (row >> 6) & 3
     side = (row >> 8) ^ core
     back_even = jnp.where(slot == 0, 3 * source, 2 - source)
     back_odd = jnp.where(slot == 0, 1 - source, 3 - source)
@@ -68,11 +68,10 @@
 
 def pieces_kernel(latent_ref, back1_ref, back2_ref, out_ref):
     rows = latent_ref.shape[0]
-    chips_lo = out_ref.shape[0] // 2
     own, back1 = latent_ref[...], back1_ref[...]
     to_even = jnp.where(lax.axis_index("hi") == 1, back2_ref[...], own)
-    for i in range(2 * chips_lo):
-        out_ref[i, :rows] = to_even if i < chips_lo else own
+    for i in range(out_ref.shape[0]):
+        out_ref[i, :rows] = to_even if i % 2 == 0 else own
         out_ref[i, rows:] = back1
 
 
@@ -131,10 +130,9 @@
 
 
 def owners_kernel(parts_ref, local_ref, to_back1_ref, to_back2_ref):
-    chips_lo = parts_ref.shape[0] // 2
     rows = local_ref.shape[0]
-    even = [parts_ref[i].astype(F32) for i in range(chips_lo)]
-    odd = [parts_ref[chips_lo + i].astype(F32) for i in range(chips_lo)]
+    parts = [parts_ref[i].astype(F32) for i in range(parts_ref.shape[0])]
+    even, odd = parts[0::2], parts[1::2]
     even, odd = sum(even[1:], even[0]), sum(odd[1:], odd[0])
     to_back1_ref[...] = (even[rows:] + odd[rows:]).astype(BF16)
     to_back2_ref[...] = even[:rows].astype(BF16)
@@ -182,7 +180,7 @@
         flops=4 << 30,
         nbytes=4 << 20,
     )(staged, back1, back2)
-    mine = lax.all_to_all(pieces, ("hi", "lo"), 0, 0, tiled=True).reshape(half, width)
+    mine = lax.all_to_all(pieces, ("lo", "hi"), 0, 0, tiled=True).reshape(half, width)
     swap = [(0, 1), (1, 0)]
     mate = lax.ppermute(mine, "core", swap)
     send, ds, wt = call(
@@ -202,7 +200,7 @@
         nbytes=4 << 20,
     )(mine, mate, ds, wt, ql, g, key_up)
     (summed,) = call(add_kernel, [((half, width), BF16)], [VMEM] * 2)(own, arrived)
-    parts = lax.all_to_all(summed.reshape(chips, 2 * rows, width), ("hi", "lo"), 0, 0, tiled=True)
+    parts = lax.all_to_all(summed.reshape(chips, 2 * rows, width), ("lo", "hi"), 0, 0, tiled=True)
     local, to_back1, to_back2 = call(
         owners_kernel,
         [((rows, width), F32), ((rows, width), BF16), ((rows, width), BF16)],

time: 77 us -> 75.1 us (0.975)
  blocking collectives: 48.9 us -> 47 us
    all_to_all x2, blocking collectives: 48.9 us -> 47 us  [the longest x1 31.4 us: on_device(): lax.all_to_all(pieces, ('lo', 'hi'), 0, 0, tiled=True).reshape(half, width)]
where the time goes in v3:
time: 75.1 us; the launch traced here: 74.7 us
  blocking collectives  47 us (63%)
  starting transfers between devices  11.5 us (15%)
  Pallas kernels  8.77 us (12%)
  waiting for transfers between devices  5.23 us (7%)
  between operations  0.8 us (1%)
  local copies, waits for them, and re-layouts  0.76 us (1%)
    all_to_all x1, blocking collectives, on_device(): lax.all_to_all(pieces, ('lo', 'hi'), 0, 0, tiled=True).reshape(half, width)  31.4 us
    all_to_all x1, blocking collectives, on_device(): lax.all_to_all(summed.reshape(chips, 2 * rows, width), ('lo', 'hi'), 0, 0...  15.6 us
    ppermute x1, waiting for transfers between devices, on_device(): lax.ppermute(latent, 'col', [(i, i + 1) for i in range(columns - 1)])  4.82 us
    ppermute x1, starting transfers between devices, on_device(): lax.ppermute(latent, 'col', [(i, i + 1) for i in range(columns - 1)])  3.6 us
    pallas_call x1, Pallas kernels, on_device(): call(attend_kernel, [((half, width), BF16), ((window, total), BF16), ((wi...  3.28 us
    ppermute x1, starting transfers between devices, on_device(): arrived = lax.ppermute(send, 'core', swap)  2.4 us
    pallas_call x1, Pallas kernels, on_device(): call(query_kernel, [((group, heads * NOPE), F32), ((group, heads * ROPE),...  2.36 us
    ppermute x1, starting transfers between devices, on_device(): lax.ppermute(to_back1, 'col', [(i + 1, i) for i in range(columns - 1)])  2.24 us
  transfers between devices with their start and end apart: 6, of which 2 were waited for; matrix products, arithmetic and copies ran while one was open for 0% of the time, Pallas kernels for 7%

profile of v3, /device:TPU:8, one launch (start us, length us, event | category | flops | bytes accessed | tf_op | source)
XLA Modules:
  0.0 74.7 jit_solution(8656006285181833641)
XLA Ops:
  0.6 0.7 collective-permute-start.1
  1.3 3.6 %collective-permute-start = (bf16[16,576]{1,0:T(8,128)(2,1)}, bf16[16,576]{1,0:T(8,128)(2,1)S(1)}, u32[]{:S(2)}, u32[]{:S(2)}) collective-permute-start(bf16[16,576]{1,0:T(8,128)(2,1)} %in_ref.1), channel_id=1, source_target_pairs={{0,16},{16,32},{32,48},{48,64},{64,80},{80,96},{96,112},{112,128},... | collective-permute-start | bytes 55304 | tf_op jit(solution)/shard_map/ppermute | solution.py:165
  4.9 0.7 copy-done.6
  5.7 0.0 copy-start.5
  5.7 0.0 collective-permute-done.1.back2_ref
  5.7 4.8 %collective-permute-done.back1_ref = bf16[16,576]{1,0:T(8,128)(2,1)S(1)} collective-permute-done((bf16[16,576]{1,0:T(8,128)(2,1)}, bf16[16,576]{1,0:T(8,128)(2,1)S(1)}, u32[]{:S(2)}, u32[]{:S(2)}) %collective-permute-start) | collective-permute-done | bytes 18464 | tf_op jit(solution)/shard_map/ppermute | solution.py:165
  10.5 31.4 %all_to_all.10 = bf16[8,32,576]{2,1,0:T(8,128)(2,1)S(1)} all-to-all(bf16[8,32,576]{2,1,0:T(8,128)(2,1)S(1)} %shard_map.95), channel_id=1, replica_groups=mesh['col'=64,'hi'=2,'lo'=4,'core'=2] {'lo','hi'}, dimensions={0} | all-to-all | bytes 589824 | tf_op jit(solution)/shard_map/all_to_all | solution.py:183
  41.9 1.9 %collective-permute-start.2 = (bf16[256,576]{1,0:T(8,128)(2,1)S(1)}, bf16[256,576]{1,0:T(8,128)(2,1)S(1)}, u32[]{:S(2)}, u32[]{:S(2)}) collective-permute-start(bf16[256,576]{1,0:T(8,128)(2,1)S(1)} %bitcast.5), channel_id=1, source_target_pairs={{0,1},{1,0},{2,3},{3,2},{4,5},{5,4},{6,7},{7,6},{8,9},{9,8},{10,11... | collective-permute-start | bytes 884744 | tf_op jit(solution)/shard_map/ppermute | solution.py:185
  43.9 0.1 pad_add_fusion.where_ref
  43.9 0.0 copy-done.4
  44.0 1.7 %shard_map.96 = (bf16[1024,576]{1,0:T(8,128)(2,1)S(1)}, bf16[1024,512]{1,0:T(8,128)(2,1)S(1)}, f32[512,128]{1,0:T(8,128)S(1)}) custom-call(s32[3]{0:T(128)S(1)} %pad_add_fusion.where_ref, s32[1,3]{1,0:T(1,128)S(1)} %copy-done.5, bf16[128,1024]{1,0:T(8,128)(2,1)S(1)} %copy-done.2, bf16[128,512]{1,0:T(8,128)(2,1)S(1)} %copy-done.4, ...), custom_call_target="tpu_custom_call" | custom-call | flops 268435456 | bytes 5242880 | tf_op jit(solution)/shard_map/pallas_call | solution.py:168
  45.7 0.0 collective-permute-done.2.mate_ref
  45.7 3.3 %shard_map.97 = (bf16[256,576]{1,0:T(8,128)(2,1)S(1)}, bf16[512,1024]{1,0:T(8,128)(2,1)S(1)}, bf16[512,1024]{1,0:T(8,128)(2,1)S(1)}) custom-call(bf16[256,576]{1,0:T(8,128)(2,1)S(1)} %bitcast.6, bf16[256,576]{1,0:T(8,128)(2,1)S(1)} %collective-permute-done.2.mate_ref, bf16[1024,576]{1,0:T(8,128)(2,1)S(1)} %get-tuple-element.17.ql_ref, ...), custom_call_target="tpu_custom_call" | custom-call | flops 1811939328 | bytes 5242880 | tf_op jit(solution)/shard_map/pallas_call | solution.py:186
  49.0 2.4 %collective-permute-start.3 = (bf16[256,576]{1,0:T(8,128)(2,1)S(1)}, bf16[256,576]{1,0:T(8,128)(2,1)S(1)}, u32[]{:S(2)}, u32[]{:S(2)}) collective-permute-start(bf16[256,576]{1,0:T(8,128)(2,1)S(1)} %get-tuple-element.27), channel_id=1, source_target_pairs={{0,1},{1,0},{2,3},{3,2},{4,5},{5,4},{6,7},{7,6},{8,9},{9,8},{10,11... | collective-permute-start | bytes 884744 | tf_op jit(solution)/shard_map/ppermute | solution.py:194
  51.4 1.3 %shard_map.98 = (f32[256,576]{1,0:T(8,128)S(1)}, f32[128,256]{1,0:T(8,128)S(1)}, f32[128,128]{1,0:T(8,128)S(1)}) custom-call(bf16[256,576]{1,0:T(8,128)(2,1)S(1)} %bitcast.7, bf16[256,576]{1,0:T(8,128)(2,1)S(1)} %collective-permute-done.2.mate_ref, bf16[512,1024]{1,0:T(8,128)(2,1)S(1)} %get-tuple-element.20.ds_ref, ...), custom_call_target="tpu_custom_call" | custom-call | flops 603979776 | bytes 4194304 | tf_op jit(solution)/shard_map/pallas_call | solution.py:195
  52.7 0.0 collective-permute-done.3.arrived_ref
  52.7 0.1 shard_map.100
  52.8 15.6 %all_to_all.11.parts_ref = bf16[8,32,576]{2,1,0:T(8,128)(2,1)S(1)} all-to-all(bf16[8,32,576]{2,1,0:T(8,128)(2,1)S(1)} %bitcast.9), channel_id=1, replica_groups=mesh['col'=64,'hi'=2,'lo'=4,'core'=2] {'lo','hi'}, dimensions={0} | all-to-all | bytes 589824 | tf_op jit(solution)/shard_map/all_to_all | solution.py:203
  68.4 2.2 %collective-permute-start.4 = (bf16[16,576]{1,0:T(8,128)(2,1)S(1)}, bf16[16,576]{1,0:T(8,128)(2,1)S(1)}, u32[]{:S(2)}, u32[]{:S(2)}) collective-permute-start(bf16[16,576]{1,0:T(8,128)(2,1)S(1)} %get-tuple-element.29), channel_id=1, source_target_pairs={{16,0},{32,16},{48,32},{64,48},{80,64},{96,80},{112,96},{128,112},... | collective-permute-start | bytes 55304 | tf_op jit(solution)/shard_map/ppermute | solution.py:217
  70.7 0.7 collective-permute-start.5
  71.4 2.4 %shard_map.99 = (f32[128,1024]{1,0:T(8,128)}, f32[128,512]{1,0:T(8,128)}) custom-call(bf16[256,576]{1,0:T(8,128)(2,1)S(1)} %bitcast.8, bf16[256,576]{1,0:T(8,128)(2,1)S(1)} %collective-permute-done.2.mate_ref, bf16[512,1024]{1,0:T(8,128)(2,1)S(1)} %get-tuple-element.20.ds_ref, bf16[512,1024]{1,0:T(8,128)(2,1)S(1)} %copy-done, ...), custom_call_target="tpu_custom_call" | custom-call | flops 738197504 | bytes 4194304 | tf_op jit(solution)/shard_map/pallas_call | solution.py:209
  73.7 0.4 collective-permute-done.4
  74.1 0.0 collective-permute-done.5
  74.1 0.6 convert_add_fusion
  (14 shorter events, 0.1 us)
Async XLA Ops:
  0.6 5.0 %collective-permute-start.1 = (bf16[16,576]{1,0:T(8,128)(2,1)}, bf16[16,576]{1,0:T(8,128)(2,1)S(1)}, u32[]{:S(2)}, u32[]{:S(2)}) collective-permute-start(bf16[16,576]{1,0:T(8,128)(2,1)} %in_ref.1), channel_id=1, source_target_pairs={{8,40},{24,56},{40,72},{56,88},{72,104},{88,120},{104,136},{120,15... | collective-permute-start | bytes 55304 | tf_op jit(solution)/shard_map/ppermute | solution.py:166
  1.3 9.2 %collective-permute-start = (bf16[16,576]{1,0:T(8,128)(2,1)}, bf16[16,576]{1,0:T(8,128)(2,1)S(1)}, u32[]{:S(2)}, u32[]{:S(2)}) collective-permute-start(bf16[16,576]{1,0:T(8,128)(2,1)} %in_ref.1), channel_id=1, source_target_pairs={{0,16},{16,32},{32,48},{48,64},{64,80},{80,96},{96,112},{112,128},... | collective-permute-start | bytes 55304 | tf_op jit(solution)/shard_map/ppermute | solution.py:165
  4.9 0.7 copy-start.6
  5.6 38.3 %copy-start.2 = (bf16[128,1024]{1,0:T(8,128)(2,1)S(1)}, bf16[128,1024]{1,0:T(8,128)(2,1)}, u32[]{:S(2)}) copy-start(bf16[128,1024]{1,0:T(8,128)(2,1)} %qn_ref.1) | copy-start | bytes 786436
  5.7 38.3 %copy-start.3 = (bf16[128,1024]{1,0:T(8,128)(2,1)S(1)}, bf16[128,1024]{1,0:T(8,128)(2,1)}, u32[]{:S(2)}) copy-start(bf16[128,1024]{1,0:T(8,128)(2,1)} %go_ref.1) | copy-start | bytes 786436
  5.7 38.3 %copy-start.4 = (bf16[128,512]{1,0:T(8,128)(2,1)S(1)}, bf16[128,512]{1,0:T(8,128)(2,1)}, u32[]{:S(2)}) copy-start(bf16[128,512]{1,0:T(8,128)(2,1)} %qr_ref.1) | copy-start | bytes 393220
  5.7 38.3 %copy-start.5 = (s32[1,3]{1,0:T(1,128)S(1)}, s32[1,3]{1,0:T(1,128)}, u32[]{:S(2)}) copy-start(s32[1,3]{1,0:T(1,128)} %keep_ref.1) | copy-start | bytes 40
  10.5 33.5 %copy-start = (bf16[512,1024]{1,0:T(8,128)(2,1)S(1)}, bf16[512,1024]{1,0:T(8,128)(2,1)}, u32[]{:S(2)}) copy-start(bf16[512,1024]{1,0:T(8,128)(2,1)} %kup_ref.5) | copy-start | bytes 3145732
  10.5 33.5 %copy-start.1 = (bf16[512,1024]{1,0:T(8,128)(2,1)S(1)}, bf16[512,1024]{1,0:T(8,128)(2,1)}, u32[]{:S(2)}) copy-start(bf16[512,1024]{1,0:T(8,128)(2,1)} %vup_ref.1) | copy-start | bytes 3145732
  41.9 3.7 %collective-permute-start.2 = (bf16[256,576]{1,0:T(8,128)(2,1)S(1)}, bf16[256,576]{1,0:T(8,128)(2,1)S(1)}, u32[]{:S(2)}, u32[]{:S(2)}) collective-permute-start(bf16[256,576]{1,0:T(8,128)(2,1)S(1)} %bitcast.5), channel_id=1, source_target_pairs={{0,1},{1,0},{2,3},{3,2},{4,5},{5,4},{6,7},{7,6},{8,9},{9,8},{10,11... | collective-permute-start | bytes 884744 | tf_op jit(solution)/shard_map/ppermute | solution.py:185
  49.0 3.7 %collective-permute-start.3 = (bf16[256,576]{1,0:T(8,128)(2,1)S(1)}, bf16[256,576]{1,0:T(8,128)(2,1)S(1)}, u32[]{:S(2)}, u32[]{:S(2)}) collective-permute-start(bf16[256,576]{1,0:T(8,128)(2,1)S(1)} %get-tuple-element.27), channel_id=1, source_target_pairs={{0,1},{1,0},{2,3},{3,2},{4,5},{5,4},{6,7},{7,6},{8,9},{9,8},{10,11... | collective-permute-start | bytes 884744 | tf_op jit(solution)/shard_map/ppermute | solution.py:194
  68.4 5.7 %collective-permute-start.4 = (bf16[16,576]{1,0:T(8,128)(2,1)S(1)}, bf16[16,576]{1,0:T(8,128)(2,1)S(1)}, u32[]{:S(2)}, u32[]{:S(2)}) collective-permute-start(bf16[16,576]{1,0:T(8,128)(2,1)S(1)} %get-tuple-element.29), channel_id=1, source_target_pairs={{16,0},{32,16},{48,32},{64,48},{80,64},{96,80},{112,96},{128,112},... | collective-permute-start | bytes 55304 | tf_op jit(solution)/shard_map/ppermute | solution.py:217
  70.7 3.4 %collective-permute-start.5 = (bf16[16,576]{1,0:T(8,128)(2,1)S(1)}, bf16[16,576]{1,0:T(8,128)(2,1)S(1)}, u32[]{:S(2)}, u32[]{:S(2)}) collective-permute-start(bf16[16,576]{1,0:T(8,128)(2,1)S(1)} %get-tuple-element.30), channel_id=1, source_target_pairs={{40,8},{56,24},{72,40},{88,56},{104,72},{120,88},{136,104},{152,12... | collective-permute-start | bytes 55304 | tf_op jit(solution)/shard_map/ppermute | solution.py:216

commit v4 on v3

--- a/solution.py
+++ b/solution.py
@@ -16,6 +16,7 @@
 SCALE = 1.0 / math.sqrt(NOPE + ROPE)
 LOG2E = 1.4426950408889634
 EARLY = 2
+PEERS = [[0, 4, 2, 6, 1, 5, 3, 7]]
 BF16 = jnp.bfloat16
 F32 = jnp.float32
 NT = (((1,), (1,)), ((), ()))
@@ -45,7 +46,7 @@
     low = row & 15
     slot = (row >> 4) & 1
     source = (row >> 5) & 1
-    lo = (row >> 6) & 3
+    lo = ((row >> 7) & 1) | ((row >> 5) & 2)
     side = (row >> 8) ^ core
     back_even = jnp.where(slot == 0, 3 * source, 2 - source)
     back_odd = jnp.where(slot == 0, 1 - source, 3 - source)
@@ -180,7 +181,7 @@
         flops=4 << 30,
         nbytes=4 << 20,
     )(staged, back1, back2)
-    mine = lax.all_to_all(pieces, ("lo", "hi"), 0, 0, tiled=True).reshape(half, width)
+    mine = lax.all_to_all(pieces, ("hi", "lo"), 0, 0, axis_index_groups=PEERS, tiled=True).reshape(half, width)
     swap = [(0, 1), (1, 0)]
     mate = lax.ppermute(mine, "core", swap)
     send, ds, wt = call(
@@ -200,7 +201,7 @@
         nbytes=4 << 20,
     )(mine, mate, ds, wt, ql, g, key_up)
     (summed,) = call(add_kernel, [((half, width), BF16)], [VMEM] * 2)(own, arrived)
-    parts = lax.all_to_all(summed.reshape(chips, 2 * rows, width), ("lo", "hi"), 0, 0, tiled=True)
+    parts = lax.all_to_all(summed.reshape(chips, 2 * rows, width), ("hi", "lo"), 0, 0, axis_index_groups=PEERS, tiled=True)
     local, to_back1, to_back2 = call(
         owners_kernel,
         [((rows, width), F32), ((rows, width), BF16), ((rows, width), BF16)],

time: 75.1 us -> 75.3 us (level)
  no operation moved by 1% of the time
where the time goes in v4:
time: 75.3 us; the launch traced here: 74.9 us
  blocking collectives  47.2 us (63%)
  starting transfers between devices  11.5 us (15%)
  Pallas kernels  8.81 us (12%)
  waiting for transfers between devices  5.21 us (7%)
  between operations  0.8 us (1%)
  local copies, waits for them, and re-layouts  0.76 us (1%)
    all_to_all x1, blocking collectives, on_device(): lax.all_to_all(pieces, ('hi', 'lo'), 0, 0, axis_index_groups=PEERS, tiled...  31.6 us
    all_to_all x1, blocking collectives, on_device(): lax.all_to_all(summed.reshape(chips, 2 * rows, width), ('hi', 'lo'), 0, 0...  15.6 us
    ppermute x1, waiting for transfers between devices, on_device(): lax.ppermute(latent, 'col', [(i, i + 1) for i in range(columns - 1)])  4.82 us
    ppermute x1, starting transfers between devices, on_device(): lax.ppermute(latent, 'col', [(i, i + 1) for i in range(columns - 1)])  3.6 us
    pallas_call x1, Pallas kernels, on_device(): call(attend_kernel, [((half, width), BF16), ((window, total), BF16), ((wi...  3.28 us
    ppermute x1, starting transfers between devices, on_device(): arrived = lax.ppermute(send, 'core', swap)  2.41 us
    pallas_call x1, Pallas kernels, on_device(): call(query_kernel, [((group, heads * NOPE), F32), ((group, heads * ROPE),...  2.38 us
    ppermute x1, starting transfers between devices, on_device(): lax.ppermute(to_back1, 'col', [(i + 1, i) for i in range(columns - 1)])  2.24 us
  transfers between devices with their start and end apart: 6, of which 2 were waited for; matrix products, arithmetic and copies ran while one was open for 0% of the time, Pallas kernels for 7%

profile of v4, /device:TPU:8, one launch (start us, length us, event | category | flops | bytes accessed | tf_op | source)
XLA Modules:
  0.0 74.9 jit_solution(1546968421416731119)
XLA Ops:
  0.6 0.7 collective-permute-start.1
  1.3 3.6 %collective-permute-start = (bf16[16,576]{1,0:T(8,128)(2,1)}, bf16[16,576]{1,0:T(8,128)(2,1)S(1)}, u32[]{:S(2)}, u32[]{:S(2)}) collective-permute-start(bf16[16,576]{1,0:T(8,128)(2,1)} %in_ref.1), channel_id=1, source_target_pairs={{0,16},{16,32},{32,48},{48,64},{64,80},{80,96},{96,112},{112,128},... | collective-permute-start | bytes 55304 | tf_op jit(solution)/shard_map/ppermute | solution.py:166
  4.9 0.7 copy-done.6
  5.7 0.0 copy-start.5
  5.7 0.0 collective-permute-done.1.back2_ref
  5.7 4.8 %collective-permute-done.back1_ref = bf16[16,576]{1,0:T(8,128)(2,1)S(1)} collective-permute-done((bf16[16,576]{1,0:T(8,128)(2,1)}, bf16[16,576]{1,0:T(8,128)(2,1)S(1)}, u32[]{:S(2)}, u32[]{:S(2)}) %collective-permute-start) | collective-permute-done | bytes 18464 | tf_op jit(solution)/shard_map/ppermute | solution.py:166
  10.5 31.6 %all_to_all.10 = bf16[8,32,576]{2,1,0:T(8,128)(2,1)S(1)} all-to-all(bf16[8,32,576]{2,1,0:T(8,128)(2,1)S(1)} %shard_map.95), channel_id=1, replica_groups={{0,8,4,12,2,10,6,14},{1,9,5,13,3,11,7,15},{16,24,20,28,18,26,22,30},{17..., dimensions={0} | all-to-all | bytes 589824 | tf_op jit(solution)/shard_map/all_to_all | solution.py:184
  42.1 1.9 %collective-permute-start.2 = (bf16[256,576]{1,0:T(8,128)(2,1)S(1)}, bf16[256,576]{1,0:T(8,128)(2,1)S(1)}, u32[]{:S(2)}, u32[]{:S(2)}) collective-permute-start(bf16[256,576]{1,0:T(8,128)(2,1)S(1)} %bitcast.5), channel_id=1, source_target_pairs={{0,1},{1,0},{2,3},{3,2},{4,5},{5,4},{6,7},{7,6},{8,9},{9,8},{10,11... | collective-permute-start | bytes 884744 | tf_op jit(solution)/shard_map/ppermute | solution.py:186
  44.0 0.1 pad_add_fusion.where_ref
  44.1 0.0 copy-done.4
  44.1 1.7 %shard_map.96 = (bf16[1024,576]{1,0:T(8,128)(2,1)S(1)}, bf16[1024,512]{1,0:T(8,128)(2,1)S(1)}, f32[512,128]{1,0:T(8,128)S(1)}) custom-call(s32[3]{0:T(128)S(1)} %pad_add_fusion.where_ref, s32[1,3]{1,0:T(1,128)S(1)} %copy-done.5, bf16[128,1024]{1,0:T(8,128)(2,1)S(1)} %copy-done.2, bf16[128,512]{1,0:T(8,128)(2,1)S(1)} %copy-done.4, ...), custom_call_target="tpu_custom_call" | custom-call | flops 268435456 | bytes 5242880 | tf_op jit(solution)/shard_map/pallas_call | solution.py:169
  45.9 0.0 collective-permute-done.2.mate_ref
  45.9 3.3 %shard_map.97 = (bf16[256,576]{1,0:T(8,128)(2,1)S(1)}, bf16[512,1024]{1,0:T(8,128)(2,1)S(1)}, bf16[512,1024]{1,0:T(8,128)(2,1)S(1)}) custom-call(bf16[256,576]{1,0:T(8,128)(2,1)S(1)} %bitcast.6, bf16[256,576]{1,0:T(8,128)(2,1)S(1)} %collective-permute-done.2.mate_ref, bf16[1024,576]{1,0:T(8,128)(2,1)S(1)} %get-tuple-element.17.ql_ref, ...), custom_call_target="tpu_custom_call" | custom-call | flops 1811939328 | bytes 5242880 | tf_op jit(solution)/shard_map/pallas_call | solution.py:187
  49.2 2.4 %collective-permute-start.3 = (bf16[256,576]{1,0:T(8,128)(2,1)S(1)}, bf16[256,576]{1,0:T(8,128)(2,1)S(1)}, u32[]{:S(2)}, u32[]{:S(2)}) collective-permute-start(bf16[256,576]{1,0:T(8,128)(2,1)S(1)} %get-tuple-element.27), channel_id=1, source_target_pairs={{0,1},{1,0},{2,3},{3,2},{4,5},{5,4},{6,7},{7,6},{8,9},{9,8},{10,11... | collective-permute-start | bytes 884744 | tf_op jit(solution)/shard_map/ppermute | solution.py:195
  51.6 1.3 %shard_map.98 = (f32[256,576]{1,0:T(8,128)S(1)}, f32[128,256]{1,0:T(8,128)S(1)}, f32[128,128]{1,0:T(8,128)S(1)}) custom-call(bf16[256,576]{1,0:T(8,128)(2,1)S(1)} %bitcast.7, bf16[256,576]{1,0:T(8,128)(2,1)S(1)} %collective-permute-done.2.mate_ref, bf16[512,1024]{1,0:T(8,128)(2,1)S(1)} %get-tuple-element.20.ds_ref, ...), custom_call_target="tpu_custom_call" | custom-call | flops 603979776 | bytes 4194304 | tf_op jit(solution)/shard_map/pallas_call | solution.py:196
  52.9 0.0 collective-permute-done.3.arrived_ref
  52.9 0.1 shard_map.100
  53.0 15.6 %all_to_all.11.parts_ref = bf16[8,32,576]{2,1,0:T(8,128)(2,1)S(1)} all-to-all(bf16[8,32,576]{2,1,0:T(8,128)(2,1)S(1)} %bitcast.9), channel_id=1, replica_groups={{0,8,4,12,2,10,6,14},{1,9,5,13,3,11,7,15},{16,24,20,28,18,26,22,30},{17..., dimensions={0} | all-to-all | bytes 589824 | tf_op jit(solution)/shard_map/all_to_all | solution.py:204
  68.6 2.2 %collective-permute-start.4 = (bf16[16,576]{1,0:T(8,128)(2,1)S(1)}, bf16[16,576]{1,0:T(8,128)(2,1)S(1)}, u32[]{:S(2)}, u32[]{:S(2)}) collective-permute-start(bf16[16,576]{1,0:T(8,128)(2,1)S(1)} %get-tuple-element.29), channel_id=1, source_target_pairs={{16,0},{32,16},{48,32},{64,48},{80,64},{96,80},{112,96},{128,112},... | collective-permute-start | bytes 55304 | tf_op jit(solution)/shard_map/ppermute | solution.py:218
  70.9 0.7 collective-permute-start.5
  71.5 2.4 %shard_map.99 = (f32[128,1024]{1,0:T(8,128)}, f32[128,512]{1,0:T(8,128)}) custom-call(bf16[256,576]{1,0:T(8,128)(2,1)S(1)} %bitcast.8, bf16[256,576]{1,0:T(8,128)(2,1)S(1)} %collective-permute-done.2.mate_ref, bf16[512,1024]{1,0:T(8,128)(2,1)S(1)} %get-tuple-element.20.ds_ref, bf16[512,1024]{1,0:T(8,128)(2,1)S(1)} %copy-done, ...), custom_call_target="tpu_custom_call" | custom-call | flops 738197504 | bytes 4194304 | tf_op jit(solution)/shard_map/pallas_call | solution.py:210
  73.9 0.4 collective-permute-done.4
  74.3 0.0 collective-permute-done.5
  74.3 0.6 convert_add_fusion
  (14 shorter events, 0.1 us)
Async XLA Ops:
  0.6 5.0 %collective-permute-start.1 = (bf16[16,576]{1,0:T(8,128)(2,1)}, bf16[16,576]{1,0:T(8,128)(2,1)S(1)}, u32[]{:S(2)}, u32[]{:S(2)}) collective-permute-start(bf16[16,576]{1,0:T(8,128)(2,1)} %in_ref.1), channel_id=1, source_target_pairs={{8,40},{24,56},{40,72},{56,88},{72,104},{88,120},{104,136},{120,15... | collective-permute-start | bytes 55304 | tf_op jit(solution)/shard_map/ppermute | solution.py:167
  1.3 9.2 %collective-permute-start = (bf16[16,576]{1,0:T(8,128)(2,1)}, bf16[16,576]{1,0:T(8,128)(2,1)S(1)}, u32[]{:S(2)}, u32[]{:S(2)}) collective-permute-start(bf16[16,576]{1,0:T(8,128)(2,1)} %in_ref.1), channel_id=1, source_target_pairs={{0,16},{16,32},{32,48},{48,64},{64,80},{80,96},{96,112},{112,128},... | collective-permute-start | bytes 55304 | tf_op jit(solution)/shard_map/ppermute | solution.py:166
  4.9 0.7 copy-start.6
  5.6 38.5 %copy-start.2 = (bf16[128,1024]{1,0:T(8,128)(2,1)S(1)}, bf16[128,1024]{1,0:T(8,128)(2,1)}, u32[]{:S(2)}) copy-start(bf16[128,1024]{1,0:T(8,128)(2,1)} %qn_ref.1) | copy-start | bytes 786436
  5.7 38.5 %copy-start.3 = (bf16[128,1024]{1,0:T(8,128)(2,1)S(1)}, bf16[128,1024]{1,0:T(8,128)(2,1)}, u32[]{:S(2)}) copy-start(bf16[128,1024]{1,0:T(8,128)(2,1)} %go_ref.1) | copy-start | bytes 786436
  5.7 38.5 %copy-start.4 = (bf16[128,512]{1,0:T(8,128)(2,1)S(1)}, bf16[128,512]{1,0:T(8,128)(2,1)}, u32[]{:S(2)}) copy-start(bf16[128,512]{1,0:T(8,128)(2,1)} %qr_ref.1) | copy-start | bytes 393220
  5.7 38.5 %copy-start.5 = (s32[1,3]{1,0:T(1,128)S(1)}, s32[1,3]{1,0:T(1,128)}, u32[]{:S(2)}) copy-start(s32[1,3]{1,0:T(1,128)} %keep_ref.1) | copy-start | bytes 40
  10.5 33.6 %copy-start = (bf16[512,1024]{1,0:T(8,128)(2,1)S(1)}, bf16[512,1024]{1,0:T(8,128)(2,1)}, u32[]{:S(2)}) copy-start(bf16[512,1024]{1,0:T(8,128)(2,1)} %kup_ref.5) | copy-start | bytes 3145732
  10.5 33.6 %copy-start.1 = (bf16[512,1024]{1,0:T(8,128)(2,1)S(1)}, bf16[512,1024]{1,0:T(8,128)(2,1)}, u32[]{:S(2)}) copy-start(bf16[512,1024]{1,0:T(8,128)(2,1)} %vup_ref.1) | copy-start | bytes 3145732
  42.1 3.8 %collective-permute-start.2 = (bf16[256,576]{1,0:T(8,128)(2,1)S(1)}, bf16[256,576]{1,0:T(8,128)(2,1)S(1)}, u32[]{:S(2)}, u32[]{:S(2)}) collective-permute-start(bf16[256,576]{1,0:T(8,128)(2,1)S(1)} %bitcast.5), channel_id=1, source_target_pairs={{0,1},{1,0},{2,3},{3,2},{4,5},{5,4},{6,7},{7,6},{8,9},{9,8},{10,11... | collective-permute-start | bytes 884744 | tf_op jit(solution)/shard_map/ppermute | solution.py:186
  49.2 3.7 %collective-permute-start.3 = (bf16[256,576]{1,0:T(8,128)(2,1)S(1)}, bf16[256,576]{1,0:T(8,128)(2,1)S(1)}, u32[]{:S(2)}, u32[]{:S(2)}) collective-permute-start(bf16[256,576]{1,0:T(8,128)(2,1)S(1)} %get-tuple-element.27), channel_id=1, source_target_pairs={{0,1},{1,0},{2,3},{3,2},{4,5},{5,4},{6,7},{7,6},{8,9},{9,8},{10,11... | collective-permute-start | bytes 884744 | tf_op jit(solution)/shard_map/ppermute | solution.py:195
  68.6 5.7 %collective-permute-start.4 = (bf16[16,576]{1,0:T(8,128)(2,1)S(1)}, bf16[16,576]{1,0:T(8,128)(2,1)S(1)}, u32[]{:S(2)}, u32[]{:S(2)}) collective-permute-start(bf16[16,576]{1,0:T(8,128)(2,1)S(1)} %get-tuple-element.29), channel_id=1, source_target_pairs={{16,0},{32,16},{48,32},{64,48},{80,64},{96,80},{112,96},{128,112},... | collective-permute-start | bytes 55304 | tf_op jit(solution)/shard_map/ppermute | solution.py:218
  70.9 3.4 %collective-permute-start.5 = (bf16[16,576]{1,0:T(8,128)(2,1)S(1)}, bf16[16,576]{1,0:T(8,128)(2,1)S(1)}, u32[]{:S(2)}, u32[]{:S(2)}) collective-permute-start(bf16[16,576]{1,0:T(8,128)(2,1)S(1)} %get-tuple-element.30), channel_id=1, source_target_pairs={{40,8},{56,24},{72,40},{88,56},{104,72},{120,88},{136,104},{152,12... | collective-permute-start | bytes 55304 | tf_op jit(solution)/shard_map/ppermute | solution.py:217
